TPU v7x, 32 devices: a whole 2x2x4 slice. The times are simulated.
32 devices in a mesh: ctx: 4 (over z), fsdp: 8 (over y, x, core).
Axes of the slice: x: 2, y: 2, z: 4, core: 2. Of those that a mesh axis runs over, the one named last changes fastest.
Arguments:
- tokens: bfloat16 [8, 1024, 2048], P('fsdp', 'ctx'), may hold values from -6 to 6
- cotangent: bfloat16 [8, 1024, 2048], P('fsdp', 'ctx'), may hold values from -6 to 6
- block_table: int32 [8], replicated, may hold values from 0 to 7, as said below
- gain_attn: float32 [2048], replicated, may hold values from 0.5 to 1.5
- w_query: bfloat16 [2048, 2048], P('fsdp'), may hold values from -0.125 to 0.125
- w_key: bfloat16 [2048, 256], P('fsdp'), may hold values from -0.125 to 0.125
- w_value: bfloat16 [2048, 256], P('fsdp'), may hold values from -0.125 to 0.125
- w_output: bfloat16 [2048, 2048], P(None, 'fsdp'), may hold values from -0.75 to 0.75
- gain_mlp: float32 [2048], replicated, may hold values from 0.5 to 1.5
- w_gate: bfloat16 [2048, 5632], P(None, 'fsdp'), may hold values from -0.125 to 0.125
- w_up: bfloat16 [2048, 5632], P(None, 'fsdp'), may hold values from -0.125 to 0.125
- w_down: bfloat16 [5632, 2048], P('fsdp'), may hold values from -0.078125 to 0.078125
Outputs:
- result: bfloat16 [8, 1024, 2048], P('fsdp', 'ctx')
- grad_tokens: bfloat16 [8, 1024, 2048], P('fsdp', 'ctx')
- grad_query: float32 [2048, 2048], P('fsdp')
- grad_key: float32 [2048, 256], P('fsdp')
- grad_value: float32 [2048, 256], P('fsdp')
- grad_output: float32 [2048, 2048], P(None, 'fsdp')
- grad_gate: float32 [2048, 5632], P(None, 'fsdp')
- grad_up: float32 [2048, 5632], P(None, 'fsdp')
- grad_down: float32 [5632, 2048], P('fsdp')
- grad_gain_attn: float32 [2048], replicated
- grad_gain_mlp: float32 [2048], replicated
Inputs may be any that keep to these rules, and one draw needn't show every extreme that they name: `block_table`: each block number 0 to 7 stands in one slot, and the two slots 2 c and 2 c + 1 hold blocks whose numbers add up to 7.
All inputs are finite; a program needn't handle non-finite values.
Results may differ from a plain program's by a relative error of at most 0.023.
Values may be sent and summed in bfloat16 or wider, within the bound.
A program may use at most 704 MiB of HBM per device.

v0:
```python
import jax
import jax.numpy as jnp
from jax import lax
from jax.sharding import PartitionSpec as P

H = 32
KV = 4
HD = 64


EPSILON = 1e-05
NEGATIVE = -1e30


def matmul(left, right):
    return jnp.dot(left, right, preferred_element_type=jnp.float32)


def across(left, right):
    return lax.dot_general(
        left, right, (((0,), (0,)), ((), ())), preferred_element_type=jnp.float32
    )


def through(left, right):
    return lax.dot_general(
        left, right, (((1,), (1,)), ((), ())), preferred_element_type=jnp.float32
    )


def angles(positions, width):
    freqs = 10000.0 ** (-jnp.arange(width // 2, dtype=jnp.float32) / (width // 2))
    turns = positions.astype(jnp.float32)[:, None] * freqs[None, :]
    turns = jnp.concatenate([turns, turns], -1)
    return (jnp.cos(turns)[:, None, :], jnp.sin(turns)[:, None, :])


def rotary(values, cosine, sine):
    middle = values.shape[-1] // 2
    turned = jnp.concatenate([-values[..., middle:], values[..., :middle]], -1)
    return values * cosine + turned * sine


def normed(hidden, gain):
    factor = lax.rsqrt(jnp.mean(hidden * hidden, -1, keepdims=True) + EPSILON)
    unit = hidden * factor
    return (unit, factor, (unit * gain).astype(jnp.bfloat16))


def normed_back(unit, factor, grad_in, gain):
    scaled = grad_in * gain
    return factor * (scaled - unit * jnp.mean(scaled * unit, -1, keepdims=True))


def split_heads(array, groups):
    count, heads, width = array.shape
    return array.reshape(count, groups, heads // groups, width).transpose(1, 0, 2, 3)


def join_heads(array):
    groups, count, inner, width = array.shape
    return array.transpose(1, 0, 2, 3).reshape(count, groups * inner, width)


def attend(queries, keys_all, values_all, pos_rows, pos_keys):
    scale = queries.shape[-1] ** (-0.5)
    allowed = pos_rows[:, None] >= pos_keys[None, :]
    q_split = split_heads(queries, KV)
    k_split = keys_all.transpose(1, 0, 2)
    v_split = values_all.transpose(1, 0, 2)

    def single(item):
        q_part, k_part, v_part = item
        scores = (
            jnp.einsum("rgd,ld->grl", q_part, k_part, preferred_element_type=jnp.float32) * scale
        )
        scores = jnp.where(allowed[None], scores, NEGATIVE)
        peak = jnp.max(scores, -1, keepdims=True)
        logsum = peak + jnp.log(jnp.sum(jnp.exp(scores - peak), -1, keepdims=True))
        probs = jnp.exp(scores - logsum).astype(jnp.bfloat16)
        mixed = jnp.einsum("grl,ld->rgd", probs, v_part, preferred_element_type=jnp.float32)
        return (mixed.astype(jnp.bfloat16), logsum)

    mixed, logsum = lax.map(single, (q_split, k_split, v_split))
    return (join_heads(mixed), logsum)


def attend_back(queries, keys_all, values_all, mixed, grad_mixed, logsum, pos_rows, pos_keys):
    scale = queries.shape[-1] ** (-0.5)
    allowed = pos_rows[:, None] >= pos_keys[None, :]
    q_split = split_heads(queries, KV)
    o_split = split_heads(mixed, KV)
    g_split = split_heads(grad_mixed, KV)
    k_split = keys_all.transpose(1, 0, 2)
    v_split = values_all.transpose(1, 0, 2)

    def single(item):
        q_part, k_part, v_part, o_part, g_part, l_part = item
        scores = (
            jnp.einsum("rgd,ld->grl", q_part, k_part, preferred_element_type=jnp.float32) * scale
        )
        scores = jnp.where(allowed[None], scores, NEGATIVE)
        probs = jnp.exp(scores - l_part)
        rounded = probs.astype(jnp.bfloat16)
        dprob = jnp.einsum("rgd,ld->grl", g_part, v_part, preferred_element_type=jnp.float32)
        delta = jnp.sum(g_part.astype(jnp.float32) * o_part.astype(jnp.float32), -1).T[:, :, None]
        dscore = (probs * (dprob - delta) * scale).astype(jnp.bfloat16)
        grad_q = jnp.einsum("grl,ld->rgd", dscore, k_part, preferred_element_type=jnp.float32)
        grad_k = jnp.einsum("grl,rgd->ld", dscore, q_part, preferred_element_type=jnp.float32)
        grad_v = jnp.einsum("grl,rgd->ld", rounded, g_part, preferred_element_type=jnp.float32)
        return (grad_q, grad_k, grad_v)

    grad_q, grad_k, grad_v = lax.map(single, (q_split, k_split, v_split, o_split, g_split, logsum))
    return (join_heads(grad_q), grad_k.transpose(1, 0, 2), grad_v.transpose(1, 0, 2))


def gate_back(grad_hidden, gate, up):
    sigma = jax.nn.sigmoid(gate)
    activated = gate * sigma
    grad_gate_in = (grad_hidden * up * sigma * (1.0 + gate * (1.0 - sigma))).astype(jnp.bfloat16)
    grad_up_in = (grad_hidden * activated).astype(jnp.bfloat16)
    return (grad_gate_in, grad_up_in)


def shards(
    tokens,
    cotangent,
    block_table,
    gain_attn,
    w_query,
    w_key,
    w_value,
    w_output,
    gain_mlp,
    w_gate,
    w_up,
    w_down,
):
    rows_in = tokens[0]
    grad_out = cotangent[0]
    count = rows_in.shape[0]
    block = count // 2
    ctx_index = lax.axis_index("ctx")
    offsets = jnp.arange(block, dtype=jnp.int32)
    owned = lax.dynamic_slice_in_dim(block_table, 2 * ctx_index, 2)
    pos_rows = (owned[:, None] * block + offsets[None, :]).reshape(-1)
    pos_keys = (block_table[:, None] * block + offsets[None, :]).reshape(-1)
    cosine, sine = angles(pos_rows, HD)
    full_query, full_key, full_value, full_output = (
        lax.all_gather(w_query, "fsdp", axis=0, tiled=True),
        lax.all_gather(w_key, "fsdp", axis=0, tiled=True),
        lax.all_gather(w_value, "fsdp", axis=0, tiled=True),
        lax.all_gather(w_output, "fsdp", axis=1, tiled=True),
    )
    inputs = rows_in.astype(jnp.float32)
    unit_one, factor_one, normal_one = normed(inputs, gain_attn)
    queries = rotary(matmul(normal_one, full_query).reshape(count, H, HD), cosine, sine).astype(
        jnp.bfloat16
    )
    keys_own = (
        rotary(matmul(normal_one, full_key).reshape(count, KV, HD), cosine, sine)
        .astype(jnp.bfloat16)
        .reshape(count, KV * HD)
    )
    values_own = matmul(normal_one, full_value).astype(jnp.bfloat16)
    keys_flat, values_flat = (
        lax.all_gather(keys_own, "ctx", axis=0, tiled=True),
        lax.all_gather(values_own, "ctx", axis=0, tiled=True),
    )
    keys_all = keys_flat.reshape(-1, KV, HD)
    values_all = values_flat.reshape(-1, KV, HD)
    mixed, logsum = attend(queries, keys_all, values_all, pos_rows, pos_keys)
    mixed_flat = mixed.reshape(count, H * HD)
    hidden_one = inputs + matmul(mixed_flat, full_output)
    unit_two, factor_two, normal_two = normed(hidden_one, gain_mlp)
    width = rows_in.shape[1]
    full_gate, full_up, full_down = (
        lax.all_gather(w_gate, "fsdp", axis=1, tiled=True),
        lax.all_gather(w_up, "fsdp", axis=1, tiled=True),
        lax.all_gather(w_down, "fsdp", axis=0, tiled=True),
    )
    gate = matmul(normal_two, full_gate)
    up = matmul(normal_two, full_up)
    hidden = (jax.nn.silu(gate) * up).astype(jnp.bfloat16)
    mlp_out = matmul(hidden, full_down)
    grad_hidden = through(grad_out, full_down)
    grad_gate_in, grad_up_in = gate_back(grad_hidden, gate, up)
    grad_normal_two = through(grad_gate_in, full_gate) + through(grad_up_in, full_up)
    stacked = lax.psum_scatter(
        jnp.concatenate(
            [
                across(grad_gate_in, normal_two),
                across(grad_up_in, normal_two),
                across(hidden, grad_out),
            ],
            1,
        ).astype(jnp.bfloat16),
        "fsdp",
        scatter_dimension=0,
        tiled=True,
    ).astype(jnp.float32)
    part_gate = stacked[:, :width].T
    part_up = stacked[:, width : 2 * width].T
    part_down = stacked[:, 2 * width :]
    result = (hidden_one + mlp_out).astype(jnp.bfloat16)
    grad_hidden_one = grad_out.astype(jnp.float32) + normed_back(
        unit_two, factor_two, grad_normal_two, gain_mlp
    )
    grad_mixed_in = grad_hidden_one.astype(jnp.bfloat16)
    grad_mixed = through(grad_mixed_in, full_output).astype(jnp.bfloat16).reshape(count, H, HD)
    grad_q, grad_k_all, grad_v_all = attend_back(
        queries, keys_all, values_all, mixed, grad_mixed, logsum, pos_rows, pos_keys
    )
    grad_k_own, grad_v_own = (
        lax.psum_scatter(
            grad_k_all.reshape(-1, KV * HD).astype(jnp.bfloat16),
            "ctx",
            scatter_dimension=0,
            tiled=True,
        ).astype(jnp.float32),
        lax.psum_scatter(
            grad_v_all.reshape(-1, KV * HD).astype(jnp.bfloat16),
            "ctx",
            scatter_dimension=0,
            tiled=True,
        ).astype(jnp.float32),
    )
    grad_queries = rotary(grad_q, cosine, -sine).astype(jnp.bfloat16).reshape(count, H * HD)
    grad_keys = (
        rotary(grad_k_own.reshape(count, KV, HD), cosine, -sine)
        .astype(jnp.bfloat16)
        .reshape(count, KV * HD)
    )
    grad_values = grad_v_own.astype(jnp.bfloat16)
    grad_normal_one = (
        through(grad_queries, full_query)
        + through(grad_keys, full_key)
        + through(grad_values, full_value)
    )
    grad_tokens = (
        grad_hidden_one + normed_back(unit_one, factor_one, grad_normal_one, gain_attn)
    ).astype(jnp.bfloat16)
    attn_stack = lax.psum_scatter(
        jnp.concatenate(
            [
                across(normal_one, grad_queries),
                across(normal_one, grad_keys),
                across(normal_one, grad_values),
                across(grad_mixed_in, mixed_flat),
            ],
            1,
        ).astype(jnp.bfloat16),
        "fsdp",
        scatter_dimension=0,
        tiled=True,
    ).astype(jnp.float32)
    query_cols = H * HD
    key_cols = KV * HD
    part_query = attn_stack[:, :query_cols]
    part_key = attn_stack[:, query_cols : query_cols + key_cols]
    part_value = attn_stack[:, query_cols + key_cols : query_cols + 2 * key_cols]
    part_output = attn_stack[:, query_cols + 2 * key_cols :].T
    slices = (
        lax.psum_scatter(
            part_query.astype(jnp.bfloat16), "ctx", scatter_dimension=1, tiled=True
        ).astype(jnp.float32),
        lax.psum_scatter(
            part_key.astype(jnp.bfloat16), "ctx", scatter_dimension=1, tiled=True
        ).astype(jnp.float32),
        lax.psum_scatter(
            part_value.astype(jnp.bfloat16), "ctx", scatter_dimension=1, tiled=True
        ).astype(jnp.float32),
        lax.psum_scatter(
            part_output.astype(jnp.bfloat16), "ctx", scatter_dimension=0, tiled=True
        ).astype(jnp.float32),
        lax.psum_scatter(
            part_gate.astype(jnp.bfloat16), "ctx", scatter_dimension=0, tiled=True
        ).astype(jnp.float32),
        lax.psum_scatter(
            part_up.astype(jnp.bfloat16), "ctx", scatter_dimension=0, tiled=True
        ).astype(jnp.float32),
        lax.psum_scatter(
            part_down.astype(jnp.bfloat16), "ctx", scatter_dimension=1, tiled=True
        ).astype(jnp.float32),
    )
    summed = (
        lax.all_gather(slices[0].astype(jnp.bfloat16), "ctx", axis=1, tiled=True).astype(
            jnp.float32
        ),
        lax.all_gather(slices[1].astype(jnp.bfloat16), "ctx", axis=1, tiled=True).astype(
            jnp.float32
        ),
        lax.all_gather(slices[2].astype(jnp.bfloat16), "ctx", axis=1, tiled=True).astype(
            jnp.float32
        ),
        lax.all_gather(slices[3].astype(jnp.bfloat16), "ctx", axis=0, tiled=True).astype(
            jnp.float32
        ),
        lax.all_gather(slices[4].astype(jnp.bfloat16), "ctx", axis=0, tiled=True).astype(
            jnp.float32
        ),
        lax.all_gather(slices[5].astype(jnp.bfloat16), "ctx", axis=0, tiled=True).astype(
            jnp.float32
        ),
        lax.all_gather(slices[6].astype(jnp.bfloat16), "ctx", axis=1, tiled=True).astype(
            jnp.float32
        ),
    )
    gain_one, gain_two = lax.psum(
        (jnp.sum(grad_normal_one * unit_one, 0), jnp.sum(grad_normal_two * unit_two, 0)),
        ("ctx", "fsdp"),
    )
    return (
        result[None],
        grad_tokens[None],
        summed[0],
        summed[1],
        summed[2],
        summed[3],
        summed[4],
        summed[5],
        summed[6],
        gain_one,
        gain_two,
    )


def solution(mesh):
    in_specs = (
        P("fsdp", "ctx", None),
        P("fsdp", "ctx", None),
        P(),
        P(),
        P("fsdp", None),
        P("fsdp", None),
        P("fsdp", None),
        P(None, "fsdp"),
        P(),
        P(None, "fsdp"),
        P(None, "fsdp"),
        P("fsdp", None),
    )
    out_specs = (
        P("fsdp", "ctx", None),
        P("fsdp", "ctx", None),
        P("fsdp", None),
        P("fsdp", None),
        P("fsdp", None),
        P(None, "fsdp"),
        P(None, "fsdp"),
        P(None, "fsdp"),
        P("fsdp", None),
        P(),
        P(),
    )
    return jax.shard_map(shards, mesh=mesh, in_specs=in_specs, out_specs=out_specs, check_vma=False)
```

profile of v0, /device:TPU:0, one launch (start us, length us, event | category | flops | bytes accessed | tf_op | source)
XLA Modules:
  0.0 1816.9 jit_solution(14693424907686895282)
XLA Ops:
  13.4 22.7 %all-gather.13.cloned.1.call-done = bf16[2048,256]{1,0:T(8,128)(2,1)} async-done(((bf16[256,256]{1,0:T(8,128)(2,1)}), bf16[2048,256]{1,0:T(8,128)(2,1)}) %all-gather.13.cloned.1.call-update) | async-done | bytes 1048592 | tf_op jit(solution)/shard_map/all_gather | solution.py:152
  37.8 16.1 all_gather.49
  54.9 6.6 all-gather.15.cloned.1.call-done
  65.7 16.6 all_gather.51
  82.2 35.6 %all-gather.17.cloned.1.call-done = bf16[2048,2048]{1,0:T(8,128)(2,1)} async-done(((bf16[256,2048]{1,0:T(8,128)(2,1)}), bf16[2048,2048]{1,0:T(8,128)(2,1)}) %all-gather.17.cloned.1.call-update) | async-done | bytes 8388624 | tf_op jit(solution)/shard_map/all_gather | solution.py:150
  117.8 12.4 copy.57
  130.3 5.9 fusion.91
  136.8 29.0 %while.28 = (s32[]{:T(128)}, bf16[4,256,8,64]{1,3,2,0:T(8,128)(2,1)S(1)}, f32[4,8,256,1]{2,1,3,0:T(8,128)S(1)}, bf16[4,1024,64]{1,2,0:T(8,128)(2,1)}, bf16[4,102...) while((s32[]{:T(128)}, ...), condition=%wide.region_4.5_spmd.clone, body=%wide.region_1.4_spmd.clone.sunk | while | flops 560330752 | bytes 27073640 | solution.py:84
  165.9 9.7 all-gather.19.cloned.1.call-done
  175.6 5.8 multiply_reduce_fusion.2
  183.0 110.8 %all-gather.23.cloned.1.call-done = bf16[2048,5632]{0,1:T(8,128)(2,1)} async-done(((bf16[2048,704]{0,1:T(8,128)(2,1)}), bf16[2048,5632]{0,1:T(8,128)(2,1)}) %all-gather.23.cloned.1.call-update) | async-done | bytes 23068688 | tf_op jit(solution)/shard_map/all_gather | solution.py:179
  293.8 13.8 fusion.114
  307.6 104.5 %all-gather.21.cloned.1.call-done = bf16[2048,5632]{0,1:T(8,128)(2,1)} async-done(((bf16[2048,704]{0,1:T(8,128)(2,1)}), bf16[2048,5632]{0,1:T(8,128)(2,1)}) %all-gather.21.cloned.1.call-update) | async-done | bytes 23068688 | tf_op jit(solution)/shard_map/all_gather | solution.py:178
  412.0 13.5 fusion.113
  425.5 104.9 %all-gather.25.cloned.1.call-done = bf16[5632,2048]{1,0:T(8,128)(2,1)} async-done(((bf16[704,2048]{1,0:T(8,128)(2,1)}), bf16[5632,2048]{1,0:T(8,128)(2,1)}) %all-gather.25.cloned.1.call-update) | async-done | bytes 23068688 | tf_op jit(solution)/shard_map/all_gather | solution.py:180
  530.4 16.3 multiply_convert_fusion
  546.7 14.4 fusion.115
  561.1 12.6 multiply_reduce_fusion
  581.4 48.4 %while.29 = (s32[]{:T(128)}, f32[4,256,8,64]{1,3,2,0:T(8,128)}, bf16[4,1024,64]{1,2,0:T(8,128)(2,1)}, bf16[4,1024,64]{1,2,0:T(8,128)(2,1)}, bf16[4,1024,64]{1,2,...) while((s32[]{:T(128)}, f32[4,256,8,64]{1,3,2,0:T(8,128)}, ...), condition=%wide.region_9.10_spmd.clone, body=%wide.region_7.9_spmd.clone.sunk | while | flops 1366030336 | bytes 54192408 | solution.py:113
  635.1 5.7 convolution_convert_fusion.3
  640.9 5.8 convolution_convert_fusion.4
  646.7 4.9 reduce-scatter.14.cloned.1.call-done
  655.0 18.8 %reduce-scatter.16.cloned.1.call-done = bf16[256,256]{0,1:T(8,128)(2,1)} async-done(((bf16[1024,256]{0,1:T(8,128)(2,1)}), bf16[256,256]{0,1:T(8,128)(2,1)}) %reduce-scatter.16.cloned.1.call-update) | async-done | bytes 131088 | tf_op jit(solution)/shard_map/reduce_scatter | solution.py:221
  675.2 14.5 pad_maximum_fusion.1
  690.9 17.5 convolution_convert_fusion.1
  708.4 13.8 convolution_convert_fusion.2
  722.3 13.0 convolution_convert_fusion
  735.3 49.3 %pad_maximum_fusion = bf16[5632,6144]{0,1:T(8,128)(2,1)} fusion(bf16[5632,2048]{0,1:T(8,128)(2,1)} %convolution_convert_fusion, bf16[5632,2048]{0,1:T(8,128)(2,1)} %convolution_convert_fusion.1, bf16[5632,2048]{0,1:T(8,128)(2,1)} %convolution_convert_fusion.2), kind=kLoop, calls=%fused_computation.67 | loop fusion | flops 207618048 | bytes 138412032 | tf_op jit(solution)/shard_map/concatenate | solution.py:190
  784.5 79.6 %copy.69 = bf16[5632,6144]{1,0:T(8,128)(2,1)} copy(bf16[5632,6144]{0,1:T(8,128)(2,1)} %pad_maximum_fusion) | data formatting | bytes 138412032
  868.0 397.9 %reduce-scatter.34.cloned.1.call-done = bf16[704,6144]{1,0:T(8,128)(2,1)} async-done(((bf16[5632,6144]{1,0:T(8,128)(2,1)}), bf16[704,6144]{1,0:T(8,128)(2,1)}) %reduce-scatter.34.cloned.1.call-update) | async-done | bytes 8650768
  1266.0 5.6 fusion.111
  1271.6 4.7 copy.73
  1286.4 9.5 reduce-scatter.20.cloned.1.call-done
  1295.9 28.7 %reduce-scatter.26.cloned.1.call-done = bf16[512,256]{1,0:T(8,128)(2,1)} async-done(((bf16[2048,256]{1,0:T(8,128)(2,1)}), bf16[512,256]{1,0:T(8,128)(2,1)}) %reduce-scatter.26.cloned.1.call-update) | async-done | bytes 262160 | tf_op jit(solution)/shard_map/reduce_scatter | solution.py:273
  1324.7 61.6 %reduce-scatter.32.cloned.1.call-done = bf16[704,512]{0,1:T(8,128)(2,1)} async-done(((bf16[704,2048]{0,1:T(8,128)(2,1)}), bf16[704,512]{0,1:T(8,128)(2,1)}) %reduce-scatter.32.cloned.1.call-update) | async-done | bytes 720912 | tf_op jit(solution)/shard_map/reduce_scatter | solution.py:282
  1386.4 63.0 %reduce-scatter.30.cloned.1.call-done = bf16[512,704]{1,0:T(8,128)(2,1)} async-done(((bf16[2048,704]{1,0:T(8,128)(2,1)}), bf16[512,704]{1,0:T(8,128)(2,1)}) %reduce-scatter.30.cloned.1.call-update) | async-done | bytes 720912 | tf_op jit(solution)/shard_map/reduce_scatter | solution.py:279
  1451.8 60.6 %reduce-scatter.28.cloned.1.call-done = bf16[512,704]{1,0:T(8,128)(2,1)} async-done(((bf16[2048,704]{1,0:T(8,128)(2,1)}), bf16[512,704]{1,0:T(8,128)(2,1)}) %reduce-scatter.28.cloned.1.call-update) | async-done | bytes 720912 | tf_op jit(solution)/shard_map/reduce_scatter | solution.py:276
  1512.5 5.9 fusion.116
  1518.4 12.3 fusion.70
  1534.6 40.6 %all-reduce = (f32[2048]{0:T(1024)}, f32[2048]{0:T(1024)}) all-reduce(f32[2048]{0:T(1024)S(1)} %get-tuple-element.196, f32[2048]{0:T(1024)S(1)} %copy-done.40), channel_id=1, replica_groups=mesh['ctx'=4,'fsdp'=8] {'ctx','fsdp'}, use_global_device_ids=true, to_apply=%region_23.24 | all-reduce | flops 4096 | bytes 32768 | tf_op jit(solution)/shard_map/psum | solution.py:309
  1578.3 13.6 all_gather.59
  1592.8 14.6 all_gather.58
  1615.5 61.9 %all-gather.35.cloned.1.call-done = bf16[704,2048]{0,1:T(8,128)(2,1)} async-done(((bf16[704,512]{0,1:T(8,128)(2,1)}), bf16[704,2048]{0,1:T(8,128)(2,1)}) %all-gather.35.cloned.1.call-update) | async-done | bytes 2883600 | tf_op jit(solution)/shard_map/all_gather | solution.py:305
  1677.4 5.2 copy.64
  1682.6 58.5 %all-gather.33.cloned.1.call-done = bf16[2048,704]{1,0:T(8,128)(2,1)} async-done(((bf16[512,704]{1,0:T(8,128)(2,1)}), bf16[2048,704]{1,0:T(8,128)(2,1)}) %all-gather.33.cloned.1.call-update) | async-done | bytes 2883600 | tf_op jit(solution)/shard_map/all_gather | solution.py:302
  1741.1 5.2 copy.63
  1746.3 58.6 %all-gather.31.cloned.1.call-done = bf16[2048,704]{1,0:T(8,128)(2,1)} async-done(((bf16[512,704]{1,0:T(8,128)(2,1)}), bf16[2048,704]{1,0:T(8,128)(2,1)}) %all-gather.31.cloned.1.call-update) | async-done | bytes 2883600 | tf_op jit(solution)/shard_map/all_gather | solution.py:299
  1804.9 5.2 copy.62
  (273 shorter events, 143.3 us)
Async XLA Ops:
  7.2 28.9 %all-gather.13.cloned.1.call-start = ((), (), s32[]{:S(2)}) async-start(), calls=%async_computation.11 | async-start | bytes 1179648 | tf_op jit(solution)/shard_map/all_gather | solution.py:152
  7.9 53.6 %all-gather.15.cloned.1.call-start = ((), (), s32[]{:S(2)}) async-start(), calls=%async_computation.12 | async-start | bytes 1179648 | tf_op jit(solution)/shard_map/all_gather | solution.py:151
  8.7 109.2 %all-gather.17.cloned.1.call-start = ((), (), s32[]{:S(2)}) async-start(), calls=%async_computation.13 | async-start | bytes 9437184 | tf_op jit(solution)/shard_map/all_gather | solution.py:150
  9.4 166.2 %all-gather.19.cloned.1.call-start = ((), (), s32[]{:S(2)}) async-start(), calls=%async_computation.14 | async-start | bytes 9437184 | tf_op jit(solution)/shard_map/all_gather | solution.py:153
  10.0 283.8 %all-gather.23.cloned.1.call-start = ((), (), s32[]{:S(2)}) async-start(), calls=%async_computation.16 | async-start | bytes 25952256 | tf_op jit(solution)/shard_map/all_gather | solution.py:179
  10.6 25.5 %copy-start.33 = (f32[2048]{0:T(1024)S(1)}, f32[2048]{0:T(1024)}, u32[]{:S(2)}) copy-start(f32[2048]{0:T(1024)} %param.19) | copy-start | bytes 24580
  10.6 401.4 %all-gather.21.cloned.1.call-start = ((), (), s32[]{:S(2)}) async-start(), calls=%async_computation.15 | async-start | bytes 25952256 | tf_op jit(solution)/shard_map/all_gather | solution.py:178
  11.2 519.2 %all-gather.25.cloned.1.call-start = ((), (), s32[]{:S(2)}) async-start(), calls=%async_computation.17 | async-start | bytes 25952256 | tf_op jit(solution)/shard_map/all_gather | solution.py:180
  11.9 639.7 %reduce-scatter.14.cloned.1.call-start = ((), (), s32[]{:S(2)}) async-start(), calls=%async_computation.18 | async-start | bytes 655360 | tf_op jit(solution)/shard_map/reduce_scatter | solution.py:215
  13.0 123.3 %copy-start.21 = (f32[256,64]{0,1:T(8,128)}, f32[256,64]{0,1:T(8,128)S(1)}, u32[]{:S(2)}) copy-start(f32[256,64]{0,1:T(8,128)S(1)} %get-tuple-element.264) | copy-start | bytes 196612
  13.4 116.9 %copy-start.37 = (f32[256]{0:T(256)}, f32[256]{0:T(256)S(1)}, u32[]{:S(2)}) copy-start(f32[256]{0:T(256)S(1)} %add_rsqrt_fusion.1) | copy-start | bytes 3076
  175.6 7.2 copy-start.36
  183.0 229.0 %copy-start.12 = (bf16[256,2048]{1,0:T(8,128)(2,1)}, bf16[256,2048]{1,0:T(8,128)(2,1)S(1)}, u32[]{:S(2)}) copy-start(bf16[256,2048]{1,0:T(8,128)(2,1)S(1)} %multiply_convert_fusion.3) | copy-start | bytes 3145732
  546.7 14.4 copy-start.19
  546.7 14.4 copy-start.20
  546.7 14.4 copy-start.7
  546.7 29.0 %slice-start = ((s8[8388608]{0:T(1024)(128)(4,1)}), s8[4194304]{0:T(1024)(128)(4,1)S(1)}, s32[]{:S(2)}) async-start(s8[8388608]{0:T(1024)(128)(4,1)} %bitcast.321), calls=%async_computation.34 | async-start | bytes 8388608
  561.1 12.7 copy-start.16
  561.1 14.6 slice-start.1
  575.7 5.7 copy-start.11
  598.3 4.2 copy-start.28
  629.8 44.0 %reduce-scatter.16.cloned.1.call-start = ((), (), s32[]{:S(2)}) async-start(), calls=%async_computation.19 | async-start | bytes 655360 | tf_op jit(solution)/shard_map/reduce_scatter | solution.py:221
  635.1 5.7 copy-start.1
  635.1 5.7 copy-start.34
  635.1 5.8 copy-start.38
  640.8 223.4 %reduce-scatter.18.cloned.1.call-start = ((), (), s32[]{:S(2)}) async-start(), calls=%async_computation.20 | async-start | bytes 21233664 | tf_op jit(solution)/shard_map/reduce_scatter | solution.py:243
  654.4 35.3 %copy-start.30 = (bf16[256,256]{0,1:T(8,128)(2,1)}, bf16[256,256]{0,1:T(8,128)(2,1)S(1)}, u32[]{:S(2)}) copy-start(bf16[256,256]{0,1:T(8,128)(2,1)S(1)} %fusion.100) | copy-start | bytes 393220
  689.7 576.2 %reduce-scatter.34.cloned.1.call-start = ((), (), s32[]{:S(2)}) async-start(), calls=%async_computation.33 | async-start | bytes 77856768
  708.4 13.8 copy-start.17
  864.1 431.7 %reduce-scatter.20.cloned.1.call-start = ((), (), s32[]{:S(2)}) async-start(), calls=%async_computation.21 | async-start | bytes 1310720 | tf_op jit(solution)/shard_map/reduce_scatter | solution.py:264
  867.2 457.4 %reduce-scatter.26.cloned.1.call-start = ((), (), s32[]{:S(2)}) async-start(), calls=%async_computation.25 | async-start | bytes 1310720 | tf_op jit(solution)/shard_map/reduce_scatter | solution.py:273
  868.0 518.3 %reduce-scatter.32.cloned.1.call-start = ((), (), s32[]{:S(2)}) async-start(), calls=%async_computation.31 | async-start | bytes 3932160 | tf_op jit(solution)/shard_map/reduce_scatter | solution.py:282
  1276.3 173.1 %reduce-scatter.30.cloned.1.call-start = ((), (), s32[]{:S(2)}) async-start(), calls=%async_computation.29 | async-start | bytes 3932160 | tf_op jit(solution)/shard_map/reduce_scatter | solution.py:279
  1281.0 231.5 %reduce-scatter.28.cloned.1.call-start = ((), (), s32[]{:S(2)}) async-start(), calls=%async_computation.27 | async-start | bytes 3932160 | tf_op jit(solution)/shard_map/reduce_scatter | solution.py:276
  1283.8 165.9 %copy-start.10 = (f32[4,256,8,64]{1,3,2,0:T(8,128)S(1)}, f32[4,256,8,64]{1,3,2,0:T(8,128)}, u32[]{:S(2)}) copy-start(f32[4,256,8,64]{1,3,2,0:T(8,128)} %get-tuple-element.110) | copy-start | bytes 6291460
  1283.8 165.9 %copy-start.23 = (f32[256,64]{0,1:T(8,128)S(1)}, f32[256,64]{0,1:T(8,128)}, u32[]{:S(2)}) copy-start(f32[256,64]{0,1:T(8,128)} %copy-done.21) | copy-start | bytes 196612
  1283.8 294.5 %reduce-scatter.24.cloned.1.call-start = ((), (), s32[]{:S(2)}) async-start(), calls=%async_computation.24 | async-start | bytes 163840 | tf_op jit(solution)/shard_map/reduce_scatter | solution.py:270
  1285.7 307.0 %reduce-scatter.22.cloned.1.call-start = ((), (), s32[]{:S(2)}) async-start(), calls=%async_computation.23 | async-start | bytes 163840 | tf_op jit(solution)/shard_map/reduce_scatter | solution.py:267
  1286.3 321.9 %all-gather.27.cloned.1.call-start = ((), (), s32[]{:S(2)}) async-start(), calls=%async_computation.22 | async-start | bytes 1310720 | tf_op jit(solution)/shard_map/all_gather | solution.py:287
  1295.9 316.9 %all-gather.29.cloned.1.call-start = ((), (), s32[]{:S(2)}) async-start(), calls=%async_computation.26 | async-start | bytes 1310720 | tf_op jit(solution)/shard_map/all_gather | solution.py:296
  1324.7 352.7 %all-gather.35.cloned.1.call-start = ((), (), s32[]{:S(2)}) async-start(), calls=%async_computation.32 | async-start | bytes 3932160 | tf_op jit(solution)/shard_map/all_gather | solution.py:305
  1386.4 354.8 %all-gather.33.cloned.1.call-start = ((), (), s32[]{:S(2)}) async-start(), calls=%async_computation.30 | async-start | bytes 3932160 | tf_op jit(solution)/shard_map/all_gather | solution.py:302
  1449.4 355.5 %all-gather.31.cloned.1.call-start = ((), (), s32[]{:S(2)}) async-start(), calls=%async_computation.28 | async-start | bytes 3932160 | tf_op jit(solution)/shard_map/all_gather | solution.py:299
  1512.4 5.9 copy-start.8
  1512.5 5.9 copy-start.18
  1518.4 12.3 copy-start.15
  1518.4 12.3 copy-start.31
  1532.2 42.9 %copy-start.5 = (f32[256,2048]{1,0:T(8,128)S(1)}, f32[256,2048]{1,0:T(8,128)}, u32[]{:S(2)}) copy-start(f32[256,2048]{1,0:T(8,128)} %copy-done.3) | copy-start | bytes 6291460
  (34 other events, 72.2 us)
Sparse Core Ops, SparseCore 0:
  9.9 26.1 all-gather.12
  38.0 23.4 all-gather.14
  63.4 54.3 all-gather.16
  119.6 55.9 all-gather.18
  177.3 116.4 all-gather.22
  295.5 116.4 all-gather.20
  413.9 116.4 all-gather.24
  629.9 21.6 reduce-scatter.13
  653.9 19.8 reduce-scatter.15
  689.9 124.3 reduce-scatter.17
  864.3 401.6 reduce-scatter.33
  1268.7 27.1 reduce-scatter.19
  1298.8 25.7 reduce-scatter.25
  1327.4 58.8 reduce-scatter.31
  1389.1 60.2 reduce-scatter.29
  1452.1 60.2 reduce-scatter.27
  1515.1 19.2 reduce-scatter.23
  1536.5 17.3 reduce-scatter.21
  1555.4 26.2 all-gather.26
  1583.2 29.5 all-gather.28
  1614.3 62.9 all-gather.34
  1678.9 62.1 all-gather.32
  1742.7 62.1 all-gather.30
where the time goes:
time: 1820 us
  waiting for transfers between devices  1230 us (68%)
  matrix products  232 us (13%)
  local copies, waits for them, and re-layouts  147 us (8%)
  blocking collectives  101 us (6%)
  other arithmetic  93.1 us (5%)
    unnamed x24, waiting for transfers between devices  404 us
    unnamed x88, local copies, waits for them, and re-layouts  117 us
    all_gather x1, waiting for transfers between devices, shards(): lax.all_gather(w_up, 'fsdp', axis=1, tiled=True)  111 us
    all_gather x1, waiting for transfers between devices, shards(): lax.all_gather(w_down, 'fsdp', axis=0, tiled=True)  105 us
    all_gather x1, waiting for transfers between devices, shards(): lax.all_gather(w_gate, 'fsdp', axis=1, tiled=True)  104 us
    reduce_scatter x1, waiting for transfers between devices, shards(): lax.psum_scatter(part_up.astype(jnp.bfloat16), 'ctx', scatter_dimension=0...  63 us
    all_gather x1, waiting for transfers between devices, shards(): lax.all_gather(slices[6].astype(jnp.bfloat16), 'ctx', axis=1, tiled=True)  61.9 us
    reduce_scatter x1, waiting for transfers between devices, shards(): lax.psum_scatter(part_down.astype(jnp.bfloat16), 'ctx', scatter_dimension...  61.6 us
  transfers between devices with their start and end apart: 23, of which 19 were waited for; matrix products, arithmetic and copies ran while one was open for 19% of the time, Pallas kernels for 0%

commit v1 on v0

--- a/solution.py
+++ b/solution.py
@@ -173,35 +173,25 @@
     mixed_flat = mixed.reshape(count, H * HD)
     hidden_one = inputs + matmul(mixed_flat, full_output)
     unit_two, factor_two, normal_two = normed(hidden_one, gain_mlp)
-    width = rows_in.shape[1]
-    full_gate, full_up, full_down = (
-        lax.all_gather(w_gate, "fsdp", axis=1, tiled=True),
-        lax.all_gather(w_up, "fsdp", axis=1, tiled=True),
-        lax.all_gather(w_down, "fsdp", axis=0, tiled=True),
-    )
-    gate = matmul(normal_two, full_gate)
-    up = matmul(normal_two, full_up)
+    rows_all = lax.all_gather(normal_two, "fsdp", axis=0, tiled=True)
+    grad_all = lax.all_gather(grad_out, "fsdp", axis=0, tiled=True)
+    gate = matmul(rows_all, w_gate)
+    up = matmul(rows_all, w_up)
     hidden = (jax.nn.silu(gate) * up).astype(jnp.bfloat16)
-    mlp_out = matmul(hidden, full_down)
-    grad_hidden = through(grad_out, full_down)
+    grad_hidden = through(grad_all, w_down)
     grad_gate_in, grad_up_in = gate_back(grad_hidden, gate, up)
-    grad_normal_two = through(grad_gate_in, full_gate) + through(grad_up_in, full_up)
-    stacked = lax.psum_scatter(
-        jnp.concatenate(
-            [
-                across(grad_gate_in, normal_two),
-                across(grad_up_in, normal_two),
-                across(hidden, grad_out),
-            ],
-            1,
-        ).astype(jnp.bfloat16),
+    grad_normal_two = lax.psum_scatter(
+        (through(grad_gate_in, w_gate) + through(grad_up_in, w_up)).astype(jnp.bfloat16),
         "fsdp",
         scatter_dimension=0,
         tiled=True,
     ).astype(jnp.float32)
-    part_gate = stacked[:, :width].T
-    part_up = stacked[:, width : 2 * width].T
-    part_down = stacked[:, 2 * width :]
+    mlp_out = lax.psum_scatter(
+        matmul(hidden, w_down).astype(jnp.bfloat16), "fsdp", scatter_dimension=0, tiled=True
+    ).astype(jnp.float32)
+    part_gate = across(rows_all, grad_gate_in)
+    part_up = across(rows_all, grad_up_in)
+    part_down = across(hidden, grad_all)
     result = (hidden_one + mlp_out).astype(jnp.bfloat16)
     grad_hidden_one = grad_out.astype(jnp.float32) + normed_back(
         unit_two, factor_two, grad_normal_two, gain_mlp
@@ -260,51 +250,17 @@
     part_key = attn_stack[:, query_cols : query_cols + key_cols]
     part_value = attn_stack[:, query_cols + key_cols : query_cols + 2 * key_cols]
     part_output = attn_stack[:, query_cols + 2 * key_cols :].T
-    slices = (
-        lax.psum_scatter(
-            part_query.astype(jnp.bfloat16), "ctx", scatter_dimension=1, tiled=True
-        ).astype(jnp.float32),
-        lax.psum_scatter(
-            part_key.astype(jnp.bfloat16), "ctx", scatter_dimension=1, tiled=True
-        ).astype(jnp.float32),
-        lax.psum_scatter(
-            part_value.astype(jnp.bfloat16), "ctx", scatter_dimension=1, tiled=True
-        ).astype(jnp.float32),
-        lax.psum_scatter(
-            part_output.astype(jnp.bfloat16), "ctx", scatter_dimension=0, tiled=True
-        ).astype(jnp.float32),
-        lax.psum_scatter(
-            part_gate.astype(jnp.bfloat16), "ctx", scatter_dimension=0, tiled=True
-        ).astype(jnp.float32),
-        lax.psum_scatter(
-            part_up.astype(jnp.bfloat16), "ctx", scatter_dimension=0, tiled=True
-        ).astype(jnp.float32),
-        lax.psum_scatter(
-            part_down.astype(jnp.bfloat16), "ctx", scatter_dimension=1, tiled=True
-        ).astype(jnp.float32),
-    )
-    summed = (
-        lax.all_gather(slices[0].astype(jnp.bfloat16), "ctx", axis=1, tiled=True).astype(
-            jnp.float32
-        ),
-        lax.all_gather(slices[1].astype(jnp.bfloat16), "ctx", axis=1, tiled=True).astype(
-            jnp.float32
-        ),
-        lax.all_gather(slices[2].astype(jnp.bfloat16), "ctx", axis=1, tiled=True).astype(
-            jnp.float32
-        ),
-        lax.all_gather(slices[3].astype(jnp.bfloat16), "ctx", axis=0, tiled=True).astype(
-            jnp.float32
-        ),
-        lax.all_gather(slices[4].astype(jnp.bfloat16), "ctx", axis=0, tiled=True).astype(
-            jnp.float32
-        ),
-        lax.all_gather(slices[5].astype(jnp.bfloat16), "ctx", axis=0, tiled=True).astype(
-            jnp.float32
-        ),
-        lax.all_gather(slices[6].astype(jnp.bfloat16), "ctx", axis=1, tiled=True).astype(
-            jnp.float32
-        ),
+    summed = tuple(
+        lax.psum(part.astype(jnp.bfloat16), "ctx").astype(jnp.float32)
+        for part in (
+            part_query,
+            part_key,
+            part_value,
+            part_output,
+            part_gate,
+            part_up,
+            part_down,
+        )
     )
     gain_one, gain_two = lax.psum(
         (jnp.sum(grad_normal_one * unit_one, 0), jnp.sum(grad_normal_two * unit_two, 0)),

time: 1820 us -> 1140 us (0.63)
  waiting for transfers between devices: 1230 us -> 729 us
  local copies, waits for them, and re-layouts: 147 us -> 36.6 us
  other arithmetic: 93.1 us -> 66.7 us
  blocking collectives: 101 us -> 78.3 us
  matrix products: 232 us -> 211 us
    all_gather x8 -> x2, waiting for transfers between devices: 501 us -> 90.7 us  [the longest x1 53.7 us: shards(): rows_all = lax.all_gather(normal_two, 'fsdp', axis=0, tiled=True)]
    unnamed x24 -> x12, waiting for transfers between devices: 404 us -> 3.22 us
    psum x0 -> x1, waiting for transfers between devices: none -> 318 us  [shards(): lax.psum(part.astype(jnp.bfloat16), 'ctx').astype(jnp.float32)]
    unnamed x88 -> x81, local copies, waits for them, and re-layouts: 117 us -> 11.1 us
    reduce_scatter x1, waiting for transfers between devices: 0.02 us -> 93.4 us  [shards(): lax.psum_scatter(jnp.concatenate([across(normal_one, grad_queries), acros...]
    reduce_scatter x7 -> x2, waiting for transfers between devices: 223 us -> 133 us  [the longest x1 72.6 us: shards(): lax.psum_scatter(matmul(hidden, w_down).astype(jnp.bfloat16), 'fsdp', sca...]
    concatenate x1 -> x0, other arithmetic: 49.3 us -> none  [shards(): jnp.concatenate([across(grad_gate_in, normal_two), across(grad_up_in, nor...]
    all_gather x2 -> x0, blocking collectives: 28.2 us -> none  [the longest x1 14.6 us: shards(): lax.all_gather(slices[1].astype(jnp.bfloat16), 'ctx', axis=1, tiled=True)]
  transfers between devices with their start and end apart: 23 -> 12, of which waited for: 19 -> 12; matrix products, arithmetic and copies ran while one was open for 19% -> 14% of each run, Pallas kernels for 0% -> 0%
where the time goes in v1:
time: 1140 us
  waiting for transfers between devices  729 us (64%)
  matrix products  211 us (19%)
  blocking collectives  78.3 us (7%)
  other arithmetic  66.7 us (6%)
  local copies, waits for them, and re-layouts  36.6 us (3%)
  between operations  15 us (1%)
    psum x1, waiting for transfers between devices, shards(): lax.psum(part.astype(jnp.bfloat16), 'ctx').astype(jnp.float32)  318 us
    reduce_scatter x1, waiting for transfers between devices, shards(): lax.psum_scatter(jnp.concatenate([across(normal_one, grad_queries), acros...  93.4 us
    reduce_scatter x1, waiting for transfers between devices, shards(): lax.psum_scatter(matmul(hidden, w_down).astype(jnp.bfloat16), 'fsdp', sca...  72.6 us
    reduce_scatter x1, waiting for transfers between devices, shards(): lax.psum_scatter((through(grad_gate_in, w_gate) + through(grad_up_in, w_u...  60.1 us
    dot_general x7, matrix products, through(): lax.dot_general(left, right, (((1,), (1,)), ((), ())), preferred_element_...  53.8 us
    all_gather x1, waiting for transfers between devices, shards(): rows_all = lax.all_gather(normal_two, 'fsdp', axis=0, tiled=True)  53.7 us
    dot_general x7, matrix products, matmul(): return jnp.dot(left, right, preferred_element_type=jnp.float32)  47 us
    psum x1, blocking collectives, shards(): lax.psum((jnp.sum(grad_normal_one * unit_one, 0), jnp.sum(grad_normal_two...  46.1 us
  transfers between devices with their start and end apart: 12, of which 12 were waited for; matrix products, arithmetic and copies ran while one was open for 14% of the time, Pallas kernels for 0%

profile of v1, /device:TPU:0, one launch (start us, length us, event | category | flops | bytes accessed | tf_op | source)
XLA Modules:
  0.0 1138.8 jit_solution(16763233488125956868)
XLA Ops:
  13.4 22.8 %all-gather.8.cloned.1.call-done = bf16[2048,256]{1,0:T(8,128)(2,1)} async-done(((bf16[256,256]{1,0:T(8,128)(2,1)}), bf16[2048,256]{1,0:T(8,128)(2,1)}) %all-gather.8.cloned.1.call-update) | async-done | bytes 1048592 | tf_op jit(solution)/shard_map/all_gather | solution.py:152
  38.2 16.1 %all_gather.25 = bf16[1024,256]{1,0:T(8,128)(2,1)S(1)} all-gather(bf16[256,256]{1,0:T(8,128)(2,1)S(1)} %convolution_convert_fusion.8), channel_id=1, replica_groups=mesh['ctx'=4,'fsdp'=8] {'ctx'}, dimensions={0}, use_global_device_ids=true | all-gather | bytes 655360 | tf_op jit(solution)/shard_map/all_gather | solution.py:168
  55.3 6.3 all-gather.10.cloned.1.call-done
  66.0 16.2 %all_gather.27 = bf16[1024,256]{0,1:T(8,128)(2,1)S(1)} all-gather(bf16[256,256]{0,1:T(8,128)(2,1)S(1)} %bitcast.335), channel_id=1, replica_groups=mesh['ctx'=4,'fsdp'=8] {'ctx'}, dimensions={0}, use_global_device_ids=true | all-gather | bytes 655360 | tf_op jit(solution)/shard_map/all_gather | solution.py:167
  82.3 35.6 %all-gather.12.cloned.1.call-done = bf16[2048,2048]{1,0:T(8,128)(2,1)} async-done(((bf16[256,2048]{1,0:T(8,128)(2,1)}), bf16[2048,2048]{1,0:T(8,128)(2,1)}) %all-gather.12.cloned.1.call-update) | async-done | bytes 8388624 | tf_op jit(solution)/shard_map/all_gather | solution.py:150
  117.9 12.3 %copy.40 = bf16[2048,2048]{1,0:T(8,128)(2,1)} copy(bf16[2048,2048]{0,1:T(8,128)(2,1)} %bitcast.323) | data formatting | bytes 16777216 | tf_op jit(solution)/shard_map/dot_general | solution.py:16
  130.2 6.2 fusion.100
  138.1 34.4 %while.28 = (s32[]{:T(128)}, bf16[4,256,8,64]{1,3,2,0:T(8,128)(2,1)}, f32[4,8,256,1]{2,1,3,0:T(8,128)}, bf16[4,1024,64]{1,2,0:T(8,128)(2,1)}, bf16[4,1024,64]{1,...) while((s32[]{:T(128)}, ...), condition=%wide.region_4.5_spmd.clone, body=%wide.region_1.4_spmd.clone.sunk | while | flops 560330752 | bytes 27073640 | solution.py:84
  143.0 3.7 fusion.180
  151.7 3.7 fusion.180
  160.2 3.7 fusion.180
  168.8 3.7 fusion.180
  172.5 3.1 all-gather.14.cloned.1.call-done
  175.6 6.4 multiply_reduce_fusion
  185.4 53.7 %all-gather.16.cloned.1.call-done = bf16[2048,2048]{1,0:T(8,128)(2,1)} async-done(((bf16[256,2048]{1,0:T(8,128)(2,1)}), bf16[2048,2048]{1,0:T(8,128)(2,1)}) %all-gather.16.cloned.1.call-update) | async-done | bytes 8388624 | tf_op jit(solution)/shard_map/all_gather | solution.py:176
  239.1 11.2 fusion.122
  250.3 8.0 fusion.121
  258.3 37.0 %all-gather.18.cloned.1.call-done = bf16[1,2048,2048]{2,1,0:T(8,128)(2,1)} async-done(((bf16[1,256,2048]{2,1,0:T(8,128)(2,1)}), bf16[1,2048,2048]{2,1,0:T(8,128)(2,1)}) %all-gather.18.cloned.1.call-update) | async-done | bytes 8388624 | tf_op jit(solution)/shard_map/all_gather | solution.py:177
  295.3 14.6 %multiply_convert_fusion = (bf16[2048,704]{0,1:T(8,128)(2,1)S(1)}, bf16[2048,704]{0,1:T(8,128)(2,1)S(1)}, bf16[2048,704]{0,1:T(8,128)(2,1)}) fusion(f32[2048,704]{0,1:T(8,128)} %fusion.121, f32[2048,704]{0,1:T(8,128)} %fusion.122, bf16[704,2048]{1,0:T(8,128)(2,1)S(1)} %copy-done, bf16[1,2048,2048]{2,1,0:T(8,128)(2,1)} %all-gather.18.cloned.1.call-done), kind=kOutput, calls=%fused_computation.76 | convolution fusion | flops 5927206912 | bytes 31457280 | tf_op jit(solution)/shard_map/dot_general | solution.py:26
  309.9 10.7 fusion.123
  320.7 12.6 %add_convert_fusion = bf16[2048,2048]{1,0:T(8,128)(2,1)} fusion(f32[2048,2048]{1,0:T(8,128)} %fusion.123, bf16[2048,704]{0,1:T(8,128)(2,1)S(1)} %get-tuple-element.240, bf16[2048,704]{0,1:T(8,128)(2,1)S(1)} %copy-done.33), kind=kOutput, calls=%fused_computation.68 | convolution fusion | flops 5913968640 | bytes 30932992 | tf_op jit(solution)/shard_map/dot_general | solution.py:26
  333.3 11.0 convolution_convert_fusion.2
  344.6 60.1 %reduce-scatter.8.cloned.1.call-done = bf16[256,2048]{1,0:T(8,128)(2,1)} async-done(((bf16[2048,2048]{1,0:T(8,128)(2,1)}), bf16[256,2048]{1,0:T(8,128)(2,1)}) %reduce-scatter.8.cloned.1.call-update) | async-done | bytes 1048592 | tf_op jit(solution)/shard_map/reduce_scatter | solution.py:183
  407.3 72.6 %reduce-scatter.6.cloned.1.call-done = bf16[256,2048]{1,0:T(8,128)(2,1)} async-done(((bf16[2048,2048]{1,0:T(8,128)(2,1)}), bf16[256,2048]{1,0:T(8,128)(2,1)}) %reduce-scatter.6.cloned.1.call-update) | async-done | bytes 1048592 | tf_op jit(solution)/shard_map/reduce_scatter | solution.py:189
  479.9 3.8 fusion.80
  484.9 6.8 convolution_convert_fusion.7
  493.3 50.1 %while.29 = (s32[]{:T(128)}, f32[4,256,8,64]{1,3,2,0:T(8,128)}, bf16[4,1024,64]{1,2,0:T(8,128)(2,1)}, bf16[4,1024,64]{1,2,0:T(8,128)(2,1)S(1)}, bf16[4,1024,64]{...) while((s32[]{:T(128)}, f32[4,256,8,64]{1,3,2,0:T(8,128)}, ...), condition=%wide.region_11.12_spmd.clone, body=%wide.region_9.11_spmd.clone.sunk | while | flops 1366030336 | bytes 45803716 | solution.py:113
  498.8 4.0 fusion.193
  511.3 4.0 fusion.193
  523.8 4.0 fusion.193
  536.4 4.0 fusion.193
  549.1 5.7 convolution_convert_fusion
  555.0 5.8 convolution_convert_fusion.1
  560.8 4.4 reduce-scatter.10.cloned.1.call-done
  568.6 18.8 %reduce-scatter.12.cloned.1.call-done = bf16[256,256]{0,1:T(8,128)(2,1)} async-done(((bf16[1024,256]{0,1:T(8,128)(2,1)}), bf16[256,256]{0,1:T(8,128)(2,1)}) %reduce-scatter.12.cloned.1.call-update) | async-done | bytes 131088 | tf_op jit(solution)/shard_map/reduce_scatter | solution.py:211
  588.8 14.4 %pad_maximum_fusion = bf16[2048,4608]{0,1:T(8,128)(2,1)} fusion(bf16[2048,2048]{0,1:T(8,128)(2,1)} %convolution_convert_fusion, bf16[2048,256]{0,1:T(8,128)(2,1)S(1)} %convolution_convert_fusion.5, bf16[2048,256]{0,1:T(8,128)(2,1)S(1)} %convolution_convert_fusion.6, bf16[2048,2048]{0,1:T(8,128)(2,1)} %convolution_convert_fusion.1), kind=kLoop, calls=%fused_computation.67 | loop fusion | flops 75497472 | bytes 37748736 | tf_op jit(solution)/shard_map/concatenate | solution.py:234
  603.6 10.7 fusion.66
  614.3 12.7 %convolution_convert_fusion.3 = bf16[2048,704]{0,1:T(8,128)(2,1)} fusion(bf16[2048,704]{0,1:T(8,128)(2,1)S(1)} %copy-done.38, bf16[2048,2048]{1,0:T(8,128)(2,1)} %all-gather.16.cloned.1.call-done), kind=kOutput, calls=%fused_computation.81 | convolution fusion | flops 5907021824 | bytes 14155776 | tf_op jit(solution)/shard_map/dot_general | solution.py:20
  627.0 7.4 convolution_convert_fusion.4
  634.4 93.4 %reduce-scatter.14.cloned.1.call-done = bf16[256,4608]{0,1:T(8,128)(2,1)} async-done(((bf16[2048,4608]{0,1:T(8,128)(2,1)}), bf16[256,4608]{0,1:T(8,128)(2,1)}) %reduce-scatter.14.cloned.1.call-update) | async-done | bytes 2359312 | tf_op jit(solution)/shard_map/reduce_scatter | solution.py:233
  729.5 3.0 slice_bitcast_fusion
  735.1 6.2 fusion.124
  744.9 46.1 %all-reduce = (f32[2048]{0:T(1024)}, f32[2048]{0:T(1024)}) all-reduce(f32[2048]{0:T(1024)S(1)} %get-tuple-element.185, f32[2048]{0:T(1024)S(1)} %copy-done.27), channel_id=1, replica_groups=mesh['ctx'=4,'fsdp'=8] {'ctx','fsdp'}, use_global_device_ids=true, to_apply=%region_24.25 | all-reduce | flops 4096 | bytes 32768 | tf_op jit(solution)/shard_map/psum | solution.py:265
  790.9 3.9 fusion.99
  794.8 318.2 %all-reduce.4.cloned.1.call-done = (bf16[256,2048]{0,1:T(8,128)(2,1)}, bf16[256,256]{0,1:T(8,128)(2,1)}, bf16[256,256]{0,1:T(8,128)(2,1)}, bf16[2048,256]{1,0:T(...) async-done(((bf16[256,2048]{0,1:T(8,128)(2,1)}, bf16[256,256]{0,1:T(8,128)(2,1)}, bf16[256,256]{0,1:T(8,128)(2,1)}, ...) | async-done | bytes 11010064 | tf_op jit(solution)/shard_map/psum | solution.py:254
  1121.7 3.3 convert_element_type.215
  1125.0 3.3 convert_element_type.217
  1128.3 3.3 convert_element_type.219
  (209 shorter events, 105.0 us)
Async XLA Ops:
  7.2 288.1 %copy-start = (bf16[704,2048]{1,0:T(8,128)(2,1)S(1)}, bf16[704,2048]{1,0:T(8,128)(2,1)}, u32[]{:S(2)}) copy-start(bf16[704,2048]{1,0:T(8,128)(2,1)} %param.27) | copy-start | bytes 8650756
  7.2 6.1 copy-start.34
  7.2 29.0 %copy-start.24 = (f32[2048]{0:T(1024)S(1)}, f32[2048]{0:T(1024)}, u32[]{:S(2)}) copy-start(f32[2048]{0:T(1024)} %param.19) | copy-start | bytes 24580
  7.2 28.9 %all-gather.8.cloned.1.call-start = ((), (), s32[]{:S(2)}) async-start(), calls=%async_computation.5 | async-start | bytes 1179648 | tf_op jit(solution)/shard_map/all_gather | solution.py:152
  8.0 53.6 %all-gather.10.cloned.1.call-start = ((), (), s32[]{:S(2)}) async-start(), calls=%async_computation.6 | async-start | bytes 1179648 | tf_op jit(solution)/shard_map/all_gather | solution.py:151
  8.7 109.2 %all-gather.12.cloned.1.call-start = ((), (), s32[]{:S(2)}) async-start(), calls=%async_computation.7 | async-start | bytes 9437184 | tf_op jit(solution)/shard_map/all_gather | solution.py:150
  9.4 166.2 %all-gather.14.cloned.1.call-start = ((), (), s32[]{:S(2)}) async-start(), calls=%async_computation.8 | async-start | bytes 9437184 | tf_op jit(solution)/shard_map/all_gather | solution.py:153
  10.0 229.1 %all-gather.16.cloned.1.call-start = ((), (), s32[]{:S(2)}) async-start(), calls=%async_computation.9 | async-start | bytes 9437184 | tf_op jit(solution)/shard_map/all_gather | solution.py:176
  11.8 124.9 %copy-start.15 = (f32[256,64]{0,1:T(8,128)}, f32[256,64]{0,1:T(8,128)S(1)}, u32[]{:S(2)}) copy-start(f32[256,64]{0,1:T(8,128)S(1)} %get-tuple-element.259) | copy-start | bytes 196612
  13.3 22.8 %copy-start.28 = (f32[256]{0:T(256)}, f32[256]{0:T(256)S(1)}, u32[]{:S(2)}) copy-start(f32[256]{0:T(256)S(1)} %add_rsqrt_fusion.1) | copy-start | bytes 3076
  175.6 7.7 copy-start.26
  184.6 110.7 %all-gather.18.cloned.1.call-start = ((), (), s32[]{:S(2)}) async-start(), calls=%async_computation.15 | async-start | bytes 9437184 | tf_op jit(solution)/shard_map/all_gather | solution.py:177
  185.2 219.5 %reduce-scatter.8.cloned.1.call-start = ((), (), s32[]{:S(2)}) async-start(), calls=%async_computation.11 | async-start | bytes 9437184 | tf_op jit(solution)/shard_map/reduce_scatter | solution.py:183
  239.1 11.2 copy-start.30
  239.1 11.2 copy-start.31
  295.3 14.6 %copy-start.32 = (bf16[2048,704]{0,1:T(8,128)(2,1)S(1)}, bf16[2048,704]{0,1:T(8,128)(2,1)}, u32[]{:S(2)}) copy-start(bf16[2048,704]{0,1:T(8,128)(2,1)} %param.25) | copy-start | bytes 8650756
  309.9 10.7 copy-start.35
  309.9 10.7 copy-start.37
  309.9 10.7 copy-start.33
  333.3 146.6 %reduce-scatter.6.cloned.1.call-start = ((), (), s32[]{:S(2)}) async-start(), calls=%async_computation.10 | async-start | bytes 9437184 | tf_op jit(solution)/shard_map/reduce_scatter | solution.py:189
  344.4 60.3 %copy-start.3 = (f32[256,2048]{1,0:T(8,128)S(1)}, f32[256,2048]{1,0:T(8,128)}, u32[]{:S(2)}) copy-start(f32[256,2048]{1,0:T(8,128)} %copy-done.2) | copy-start | bytes 6291460
  344.4 220.8 %reduce-scatter.10.cloned.1.call-start = ((), (), s32[]{:S(2)}) async-start(), calls=%async_computation.12 | async-start | bytes 655360 | tf_op jit(solution)/shard_map/reduce_scatter | solution.py:205
  484.9 8.3 copy-start.5
  498.8 4.0 copy-start.21
  511.3 4.0 copy-start.21
  523.8 4.0 copy-start.21
  536.3 4.0 copy-start.21
  543.4 3.7 copy-start.20
  543.4 43.9 %reduce-scatter.12.cloned.1.call-start = ((), (), s32[]{:S(2)}) async-start(), calls=%async_computation.13 | async-start | bytes 655360 | tf_op jit(solution)/shard_map/reduce_scatter | solution.py:211
  545.4 2.2 copy-start.8
  545.4 2.2 copy-start.16
  549.1 5.8 copy-start.4
  549.1 5.8 copy-start.10
  549.1 5.8 copy-start.25
  549.1 5.8 copy-start.29
  554.9 172.9 %reduce-scatter.14.cloned.1.call-start = ((), (), s32[]{:S(2)}) async-start(), calls=%async_computation.14 | async-start | bytes 21233664 | tf_op jit(solution)/shard_map/reduce_scatter | solution.py:233
  603.2 509.8 %all-reduce.4.cloned.1.call-start = ((), (), s32[]{:S(2)}) async-start(), calls=%async_computation.16 | async-start | bytes 22020096 | tf_op jit(solution)/shard_map/psum | solution.py:254
  603.5 10.7 copy-start.38
  603.6 23.4 %slice-start = ((s8[8388608]{0:T(1024)(128)(4,1)}), s8[4194304]{0:T(1024)(128)(4,1)S(1)}, s32[]{:S(2)}) async-start(s8[8388608]{0:T(1024)(128)(4,1)} %bitcast.337), calls=%async_computation.17 | async-start | bytes 8388608
  614.3 12.7 %slice-start.1 = ((s8[8388608]{0:T(1024)(128)(4,1)}), s8[4194304]{0:T(1024)(128)(4,1)S(1)}, s32[]{:S(2)}) async-start(s8[8388608]{0:T(1024)(128)(4,1)} %bitcast.337), calls=%async_computation.18 | async-start | bytes 8388608
  614.3 12.7 %copy-start.36 = (bf16[2048,704]{0,1:T(8,128)(2,1)S(1)}, bf16[2048,704]{0,1:T(8,128)(2,1)}, u32[]{:S(2)}) copy-start(bf16[2048,704]{0,1:T(8,128)(2,1)} %copy-done.35) | copy-start | bytes 8650756
  735.1 6.3 copy-start.11
  742.6 2.3 copy-start.27
  1113.1 6.1 copy-start.18
  1119.1 2.6 copy-start.14
  1121.7 3.3 copy-start.13
  1125.0 3.3 copy-start.12
  1128.3 3.3 copy-start.1
  (11 other events, 17.6 us)
Sparse Core Ops, SparseCore 0:
  9.9 26.1 all-gather.7
  38.1 23.4 all-gather.9
  63.5 54.3 all-gather.11
  119.6 55.9 all-gather.13
  184.7 54.3 all-gather.15
  240.9 54.3 all-gather.17
  333.4 71.2 reduce-scatter.7
  408.5 71.2 reduce-scatter.5
  543.6 21.6 reduce-scatter.9
  567.3 19.9 reduce-scatter.11
  603.4 124.3 reduce-scatter.13
  732.6 380.3 all-reduce.3

commit v2 on v1

v2 whole, which is shorter than its diff:
```python
import functools

import jax
import jax.numpy as jnp
from jax import lax
from jax.experimental import pallas as pl
from jax.experimental.pallas import tpu as pltpu
from jax.sharding import PartitionSpec as P

H = 32
KV = 4
HD = 64
GROUP = H // KV
PAIRS = GROUP // 2
LANES = 128

EPSILON = 1e-05
NEGATIVE = -1e30
SLOTS = 6
VMEM_LIMIT = 60 * 1024 * 1024
MESH = pl.DeviceIdType.MESH
F32 = jnp.float32
BF16 = jnp.bfloat16


def dot(left, right, left_dim, right_dim):
    return lax.dot_general(
        left, right, (((left_dim,), (right_dim,)), ((), ())), preferred_element_type=F32
    )


def matmul(left, right):
    return dot(left, right, 1, 0)


def across(left, right):
    return dot(left, right, 0, 0)


def through(left, right):
    return dot(left, right, 1, 1)


def normed(hidden, gain):
    factor = lax.rsqrt(jnp.mean(hidden * hidden, -1, keepdims=True) + EPSILON)
    unit = hidden * factor
    return (unit, factor, (unit * gain).astype(BF16))


def normed_back(unit, factor, grad_in, gain):
    scaled = grad_in * gain
    return factor * (scaled - unit * jnp.mean(scaled * unit, -1, keepdims=True))


def gate_back(grad_hidden, gate, up):
    sigma = jax.nn.sigmoid(gate)
    activated = gate * sigma
    grad_gate_in = (grad_hidden * up * sigma * (1.0 + gate * (1.0 - sigma))).astype(BF16)
    grad_up_in = (grad_hidden * activated).astype(BF16)
    return ((activated * up).astype(BF16), grad_gate_in, grad_up_in)


def lanes_of(shape):
    return lax.broadcasted_iota(jnp.int32, shape, len(shape) - 1)


def roll_lanes(value, amount):
    return pltpu.roll(value, amount, 1)


def turned(value):
    first = lax.rem(lanes_of(value.shape), HD) < HD // 2
    return jnp.where(first, -roll_lanes(value, LANES - HD // 2), roll_lanes(value, HD // 2))


def stacked(ref, rows, group):
    wide = PAIRS * LANES
    block = ref[rows, pl.ds(pl.multiple_of(group * wide, wide), wide)]
    return jnp.concatenate([block[:, j * LANES : (j + 1) * LANES] for j in range(PAIRS)], 0)


def spread_heads(ref, out_ref, group):
    at = pl.multiple_of((group // 2) * LANES, LANES)
    tile = ref[:, pl.ds(at, LANES)].astype(F32)
    other = roll_lanes(tile, HD)
    half = lanes_of(tile.shape) // HD
    here = lax.rem(group, 2)
    for par in range(2):
        picked = jnp.where(here == par, tile, other)
        out_ref[par] = jnp.where(half == par, picked, 0.0).astype(BF16)


def attend_kernel(q_ref, k_ref, v_ref, mask_ref, o_ref, lse_ref, kz, vz):
    block = q_ref.shape[0] // 2
    keys = k_ref.shape[0] // 2
    scale = HD ** (-0.5)
    lse_ref[...] = jnp.zeros_like(lse_ref)

    def per_group(group, _):
        spread_heads(k_ref, kz, group)
        spread_heads(v_ref, vz, group)
        for rb in range(2):
            rows = pl.ds(rb * block, block)
            q4 = stacked(q_ref, rows, group) * jnp.asarray(scale, BF16)
            mask = mask_ref[rb]
            mask = jnp.concatenate([mask] * PAIRS, 0)
            total = 0.0
            lse = lse_ref[rb]
            for par in range(2):
                low = through(q4, kz[par, pl.ds(0, keys)])
                scores = [low + mask] if rb == 0 else [low]
                if rb == 1:
                    scores.append(through(q4, kz[par, pl.ds(keys, keys)]) + mask)
                peak = functools.reduce(
                    jnp.maximum, [jnp.max(s, -1, keepdims=True) for s in scores]
                )
                probs = [jnp.exp(s - peak) for s in scores]
                norm = sum(jnp.sum(p, -1, keepdims=True) for p in probs)
                mixed = sum(
                    matmul(p.astype(BF16), vz[par, pl.ds(i * keys, keys)])
                    for i, p in enumerate(probs)
                )
                total = total + mixed / norm
                lse = jnp.where(lanes_of(lse.shape) == 2 * group + par, peak + jnp.log(norm), lse)
            lse_ref[rb] = lse
            for j in range(PAIRS):
                at = pl.multiple_of((group * PAIRS + j) * LANES, LANES)
                o_ref[rows, pl.ds(at, LANES)] = total[j * block : (j + 1) * block].astype(BF16)
        return 0

    lax.fori_loop(0, KV, per_group, 0)


def attend(q, k_all, v_all, mask):
    count = q.shape[0]
    total = k_all.shape[0]
    vmem = pl.BlockSpec(memory_space=pltpu.VMEM)
    return pl.pallas_call(
        attend_kernel,
        out_shape=(
            jax.ShapeDtypeStruct((count, H * HD), BF16),
            jax.ShapeDtypeStruct((2, PAIRS * count // 2, LANES), F32),
        ),
        in_specs=[vmem] * 4,
        out_specs=(vmem, vmem),
        scratch_shapes=[
            pltpu.VMEM((2, total, LANES), BF16),
            pltpu.VMEM((2, total, LANES), BF16),
        ],
        compiler_params=pltpu.CompilerParams(vmem_limit_bytes=VMEM_LIMIT),
        cost_estimate=pl.CostEstimate(
            flops=4 * count * total * H * HD, bytes_accessed=4 << 20, transcendentals=H * count * total
        ),
        name="attend",
    )(q, k_all, v_all, mask)


class LineSum:
    def __init__(self, count, index, first, second, sources, targets, bufs, sems):
        self.n = count
        self.first, self.second = first, second
        self.total = first + second
        self.mlp_src, self.att_src = sources
        self.gate_dst, self.up_dst, self.down_dst, self.query_dst, self.output_dst = targets
        self.own, self.rout, self.sums, self.rin, self.done, self.flip = bufs
        (
            self.load_sem,
            self.in_send,
            self.rout_sem,
            self.rin_sem,
            self.out_send,
            self.store_sem,
            self.credit_in,
            self.credit_out,
        ) = sems
        half = count // 2
        left = index < half
        self.depth = jnp.where(left, index, count - 1 - index)
        step = jnp.where(left, 1, -1)
        self.inward = index + step
        outward = index - step
        self.has_out = self.depth > 0
        self.outward = jnp.where(self.has_out, outward, index + step)
        self.is_mid = self.depth == half - 1
        deepest = half - 1
        self.lag_sum = 1 + 2 * self.depth
        self.lag_sent = self.lag_sum + 2
        self.lag_total = 1 + 2 * deepest + 2 + 2 * (deepest - self.depth)
        self.lag_end = self.lag_total + 3
        self.ticks = self.total + 1 + 2 * deepest + 2 + 2 * deepest + 3
        self.att_rows = self.att_src.shape[1]
        self.blocks = self.down_dst.shape[1] // LANES

    def view(self, buf, slot, att):
        return buf.at[slot, pl.ds(0, self.att_rows)] if att else buf.at[slot]

    def each(self, chunk, body):
        slot = lax.rem(jnp.maximum(chunk, 0), SLOTS)
        pl.when((chunk >= 0) & (chunk < self.first))(lambda: body(chunk, slot, False))
        if self.second:
            pl.when((chunk >= self.first) & (chunk < self.total))(lambda: body(chunk, slot, True))

    def send(self, src, dst, sems, target, slot, att):
        return pltpu.make_async_remote_copy(
            src_ref=self.view(src, slot, att),
            dst_ref=self.view(dst, slot, att),
            send_sem=sems[0].at[slot],
            recv_sem=sems[1].at[slot],
            device_id={"ctx": target},
            device_id_type=MESH,
        )

    def to_total(self, slot, att):
        return self.send(self.sums, self.rin, (self.in_send, self.rin_sem), self.inward, slot, att)

    def to_partial(self, slot, att):
        return self.send(
            self.sums, self.rout, (self.in_send, self.rout_sem), self.inward, slot, att
        )

    def to_outward(self, slot, att):
        return self.send(
            self.done, self.rin, (self.out_send, self.rin_sem), self.outward, slot, att
        )

    def load(self, chunk, slot):
        return pltpu.make_async_copy(
            self.mlp_src.at[chunk], self.own.at[slot], self.load_sem.at[slot]
        )

    def stores(self, chunk, slot, att):
        if att:
            rows = self.att_rows // 2
            wide = self.query_dst.shape[1] // LANES
            pairs = []
            for i in range(2):
                at = 2 * (chunk - self.first) + i
                src = self.done.at[slot, pl.ds(i * rows, rows)]
                sem = self.store_sem.at[slot, i]
                q_at = pl.multiple_of(jnp.minimum(at, wide - 1) * LANES, LANES)
                o_at = pl.multiple_of(jnp.maximum(at - wide, 0) * LANES, LANES)
                pairs.append(
                    (
                        at < wide,
                        pltpu.make_async_copy(src, self.query_dst.at[:, pl.ds(q_at, LANES)], sem),
                    )
                )
                pairs.append(
                    (
                        at >= wide,
                        pltpu.make_async_copy(src, self.output_dst.at[:, pl.ds(o_at, LANES)], sem),
                    )
                )
            return pairs
        kind = chunk // self.blocks
        at = pl.multiple_of(lax.rem(chunk, self.blocks) * LANES, LANES)
        sem = self.store_sem.at[slot, 0]
        return [
            (
                kind == 0,
                pltpu.make_async_copy(self.flip.at[slot], self.gate_dst.at[pl.ds(at, LANES)], sem),
            ),
            (
                kind == 1,
                pltpu.make_async_copy(self.flip.at[slot], self.up_dst.at[pl.ds(at, LANES)], sem),
            ),
            (
                kind == 2,
                pltpu.make_async_copy(
                    self.done.at[slot], self.down_dst.at[:, pl.ds(at, LANES)], sem
                ),
            ),
        ]

    def tick(self, i):
        self.each(i - self.lag_sum + 1, self.stage_load)
        self.each(i - self.lag_sum, self.stage_sum)
        self.each(i - self.lag_sent, self.stage_sent)
        self.each(i - self.lag_total, self.stage_total)
        self.each(i - self.lag_end, self.stage_end)

    def stage_load(self, chunk, slot, att):
        if not att:
            self.load(chunk, slot).start()

    def stage_sum(self, chunk, slot, att):
        if not att:
            self.load(chunk, slot).wait()

        def own():
            return self.att_src[chunk - self.first] if att else self.own[slot]

        @pl.when(self.has_out)
        def _():
            self.to_partial(slot, att).wait_recv()
            arrived = self.view(self.rout, slot, att)[...].astype(F32)
            self.view(self.sums, slot, att)[...] = (own().astype(F32) + arrived).astype(BF16)

            @pl.when(chunk < self.total - SLOTS)
            def _():
                pl.semaphore_signal(
                    self.credit_in, 1, device_id={"ctx": self.outward}, device_id_type=MESH
                )

        @pl.when(jnp.logical_not(self.has_out))
        def _():
            self.view(self.sums, slot, att)[...] = own()

        @pl.when(chunk >= SLOTS)
        def _():
            pl.semaphore_wait(self.credit_in, 1)

        pl.when(self.is_mid)(lambda: self.to_total(slot, att).start())
        pl.when(jnp.logical_not(self.is_mid))(lambda: self.to_partial(slot, att).start())

    def stage_sent(self, chunk, slot, att):
        self.to_total(slot, att).wait_send()

    def stage_total(self, chunk, slot, att):
        self.to_total(slot, att).wait_recv()
        arrived = self.view(self.rin, slot, att)
        done = self.view(self.done, slot, att)

        @pl.when(self.is_mid)
        def _():
            mine = self.view(self.sums, slot, att)[...].astype(F32)
            done[...] = (mine + arrived[...].astype(F32)).astype(BF16)

            @pl.when(chunk < self.total - SLOTS)
            def _():
                pl.semaphore_signal(
                    self.credit_in, 1, device_id={"ctx": self.inward}, device_id_type=MESH
                )

        @pl.when(jnp.logical_not(self.is_mid))
        def _():
            done[...] = arrived[...]

            @pl.when(chunk < self.total - SLOTS)
            def _():
                pl.semaphore_signal(
                    self.credit_out, 1, device_id={"ctx": self.inward}, device_id_type=MESH
                )

        @pl.when(self.has_out)
        def _():
            @pl.when(chunk >= SLOTS)
            def _():
                pl.semaphore_wait(self.credit_out, 1)

            self.to_outward(slot, att).start()

        if not att:

            @pl.when(chunk < 2 * self.blocks)
            def _():
                self.flip[slot] = self.done[slot].T

        for condition, copy in self.stores(chunk, slot, att):
            pl.when(condition)(copy.start)

    def stage_end(self, chunk, slot, att):
        pl.when(self.has_out)(lambda: self.to_outward(slot, att).wait_send())
        for condition, copy in self.stores(chunk, slot, att):
            pl.when(condition)(copy.wait)


def chip_at(place):
    return 2 * (place // 2) + lax.rem(place + place // 2, 2)


class Ring:
    def __init__(self, count, index):
        self.chips = count // 2
        chip = index // 2
        self.core = lax.rem(index, 2)
        self.place = chip_at(chip)
        self.partner = 2 * chip + 1 - self.core
        self.right = self.device(1)
        self.left = self.device(-1)

    def device(self, offset, core=None):
        place = lax.rem(self.place + offset + self.chips, self.chips)
        return 2 * chip_at(place) + (self.core if core is None else core)


class RingSum:
    def __init__(self, ring, partial, bufs, sems):
        self.ring, self.partial = ring, partial
        self.stage, self.pair, self.from_left, self.from_right = bufs
        (
            self.stage_send,
            self.pair_recv,
            self.right_send,
            self.right_recv,
            self.left_send,
            self.left_recv,
        ) = sems
        far = ring.chips // 2
        self.far = far
        offsets = [far]
        for s in range(far - 1, 0, -1):
            offsets += [s, -s]
        self.offsets = offsets + [0]
        self.at = {offset: i for i, offset in enumerate(self.offsets)}
        self.rows = self.pair.shape[1]

    def half(self, which):
        return pl.ds(which * (self.rows // 2), self.rows // 2)

    def pair_copy(self, i):
        return pltpu.make_async_remote_copy(
            src_ref=self.stage.at[i % 2],
            dst_ref=self.pair.at[i],
            send_sem=self.stage_send.at[i],
            recv_sem=self.pair_recv.at[i],
            device_id={"fsdp": self.ring.partner},
            device_id_type=MESH,
        )

    def pair_step(self, i):
        offset = self.offsets[i]
        if i >= 2:
            self.pair_copy(i - 2).wait_send()
        self.stage[i % 2] = self.partial(self.ring.device(offset, 1 - self.ring.core)).astype(BF16)
        self.pair_copy(i).start()

    def pair_add(self, i):
        mine = self.partial(self.ring.device(self.offsets[i]))
        self.pair_copy(i).wait_recv()
        self.pair[i] = (mine + self.pair[i].astype(F32)).astype(BF16)

    def pair_all(self):
        last = len(self.offsets)
        for i in range(last):
            self.pair_step(i)
            if i >= 1:
                self.pair_add(i - 1)
        self.pair_add(last - 1)
        for i in range(max(last - 2, 0), last):
            self.pair_copy(i).wait_send()

    def hop(self, s, right, which):
        owner = self.at[s if right or s == self.far else -s]
        rows = self.half(which)
        return pltpu.make_async_remote_copy(
            src_ref=self.pair.at[owner, rows],
            dst_ref=(self.from_left if right else self.from_right).at[s - 1, rows],
            send_sem=(self.right_send if right else self.left_send).at[s - 1, which],
            recv_sem=(self.right_recv if right else self.left_recv).at[s - 1, which],
            device_id={"fsdp": self.ring.right if right else self.ring.left},
            device_id_type=MESH,
        )

    def hops(self):
        far = self.far
        moves = [(far, True, 0), (far, False, 1)]
        if far > 1:
            moves += [(far - 1, True, 1), (far - 1, False, 0)]
            moves += [(far - 1, True, 0), (far - 1, False, 1)]
        for s in range(far - 2, 0, -1):
            for which in range(2):
                moves += [(s, True, which), (s, False, which)]
        return moves

    def free(self, s, right, which):
        return s == self.far or (s == self.far - 1 and which == (1 if right else 0))

    def launch(self, free):
        for s, right, which in self.hops():
            if self.free(s, right, which) == free:
                if not free:
                    before = self.hop(s + 1, right, which)
                    before.wait_recv()
                    owner = self.at[s if right else -s]
                    rows = self.half(which)
                    arrived = (self.from_left if right else self.from_right).at[s, rows]
                    self.pair[owner, rows] = (
                        self.pair[owner, rows].astype(F32) + arrived[...].astype(F32)
                    ).astype(BF16)
                self.hop(s, right, which).start()

    def finish(self):
        for s, right, which in self.hops():
            if s == 1:
                self.hop(s, right, which).wait_recv()
            self.hop(s, right, which).wait_send()
        own = self.pair[self.at[0]].astype(F32)
        if self.far == 1:
            joined = jnp.concatenate(
                [self.from_left[0, self.half(0)], self.from_right[0, self.half(1)]], 0
            )
            return own + joined.astype(F32)
        return own + self.from_left[0].astype(F32) + self.from_right[0].astype(F32)


def back_kernel(
    sizes,
    gz_ref,
    wqkv_ref,
    q_ref,
    o_ref,
    do_ref,
    dhb_ref,
    a1_ref,
    k_ref,
    v_ref,
    lse_ref,
    mask_ref,
    turn_ref,
    x_ref,
    dh1_ref,
    gain_ref,
    gpart_ref,
    gtok_ref,
    gains_ref,
    gate_out,
    up_out,
    down_out,
    query_out,
    output_out,
    *scratch,
):
    ctx_n, fsdp_n = sizes
    (
        zown,
        zrout,
        zsums,
        zrin,
        zdone,
        zflip,
        az,
        xstage,
        xpair,
        xleft,
        xright,
        ystage,
        ypair,
        yleft,
        yright,
        kz,
        vz,
        dk_acc,
        dv_acc,
        dkv,
        dkv_in,
        gqkv,
        wbuf,
        gslot,
        cslot,
        load_sem,
        in_send,
        rout_sem,
        rin_sem,
        out_send,
        store_sem,
        credit_in,
        credit_out,
        xs0,
        xs1,
        xs2,
        xs3,
        xs4,
        xs5,
        ys0,
        ys1,
        ys2,
        ys3,
        ys4,
        ys5,
        dkv_send,
        dkv_recv,
        gain_send,
        gain_recv,
        cgain_send,
        cgain_recv,
        wsem,
    ) = scratch
    ctx = lax.axis_index("ctx")
    fsdp = lax.axis_index("fsdp")
    ring = Ring(fsdp_n, fsdp)
    count = q_ref.shape[0]
    block = count // 2
    keys = k_ref.shape[0] // 2
    scale = HD ** (-0.5)
    width = q_ref.shape[1]
    shard = query_out.shape[0]

    barrier = pltpu.get_barrier_semaphore()
    for step in range(1, ctx_n):
        pl.semaphore_signal(
            barrier,
            1,
            device_id={"ctx": lax.rem(ctx + step, ctx_n)},
            device_id_type=MESH,
        )
    for step in range(1, fsdp_n):
        pl.semaphore_signal(
            barrier,
            1,
            device_id={"fsdp": lax.rem(fsdp + step, fsdp_n)},
            device_id_type=MESH,
        )
    pl.semaphore_wait(barrier, ctx_n + fsdp_n - 2)

    line = LineSum(
        ctx_n,
        ctx,
        gz_ref.shape[0],
        az.shape[0],
        (gz_ref, az),
        (gate_out, up_out, down_out, query_out, output_out),
        (zown, zrout, zsums, zrin, zdone, zflip),
        (load_sem, in_send, rout_sem, rin_sem, out_send, store_sem, credit_in, credit_out),
    )

    clock = [0]

    def ticks(number):
        start = clock[0]
        clock[0] = start + number

        def body(i, _):
            line.tick(i)
            return 0

        lax.fori_loop(start, start + number, body, 0)

    ticks(2)

    def output_partial(f):
        return across(dhb_ref[:, pl.ds(pl.multiple_of(f * shard, shard), shard)], o_ref[...])

    ysum = RingSum(
        ring, output_partial, (ystage, ypair, yleft, yright), (ys0, ys1, ys2, ys3, ys4, ys5)
    )
    ysum.pair_all()
    ysum.launch(True)

    def piece(group, rb, par, q4, do4, lse, delta, at, mask, grad_q):
        span = pl.ds(at, keys)
        k_part = kz[par, span]
        v_part = vz[par, span]
        scores = through(q4, k_part)
        if mask is not None:
            scores = scores + mask
        probs = jnp.exp(scores - lse)
        dprob = through(do4, v_part)
        dscore = (probs * (dprob - delta)).astype(BF16)
        dk_acc[par, span] += across(dscore, q4)
        dv_acc[par, span] += across(probs.astype(BF16), do4)
        return grad_q + matmul(dscore, k_part)

    def group_step(group, rb):
        rows = pl.ds(rb * block, block)
        q4 = stacked(q_ref, rows, group) * jnp.asarray(scale, BF16)
        do4 = stacked(do_ref, rows, group)
        prod = do4.astype(F32) * stacked(o_ref, rows, group).astype(F32)
        lse_all = lse_ref[rb]
        mask = jnp.concatenate([mask_ref[rb]] * PAIRS, 0)
        grad_q = jnp.zeros((PAIRS * block, LANES), F32)
        for par in range(2):
            lse = jnp.sum(
                jnp.where(lanes_of(lse_all.shape) == 2 * group + par, lse_all, 0.0),
                -1,
                keepdims=True,
            )
            delta = jnp.sum(
                jnp.where(lanes_of(prod.shape) // HD == par, prod, 0.0), -1, keepdims=True
            )
            grad_q = piece(
                group, rb, par, q4, do4, lse, delta, 0, mask if rb == 0 else None, grad_q
            )
            if rb == 1:
                grad_q = piece(group, rb, par, q4, do4, lse, delta, keys, mask, grad_q)
        grad_q = grad_q * scale
        cosine, sine = turn_ref[0, rows], turn_ref[1, rows]
        for j in range(PAIRS):
            part = grad_q[j * block : (j + 1) * block]
            at = pl.multiple_of((group * PAIRS + j) * LANES, LANES)
            gqkv[rows, pl.ds(at, LANES)] = (part * cosine - turned(part) * sine).astype(BF16)

    def dkv_copy(owner, tile, step):
        return pltpu.make_async_remote_copy(
            src_ref=dkv.at[owner, tile],
            dst_ref=dkv_in.at[ctx, tile],
            send_sem=dkv_send.at[step, tile],
            recv_sem=dkv_recv.at[step, tile],
            device_id={"ctx": owner},
            device_id_type=MESH,
        )

    def attention(lo, hi, per_rb):
        start = clock[0]

        def body(group, _):
            spread_heads(k_ref, kz, group)
            spread_heads(v_ref, vz, group)
            dk_acc[...] = jnp.zeros_like(dk_acc)
            dv_acc[...] = jnp.zeros_like(dv_acc)
            for rb in range(2):
                group_step(group, rb)
                base = start + (group - lo) * 2 * per_rb + rb * per_rb
                for t in range(per_rb):
                    line.tick(base + t)
            tile = group // 2
            for which, acc in enumerate((dk_acc, dv_acc)):
                for part in range(ctx_n):
                    for rb in range(2):
                        span = pl.ds(rb * keys + part * block, block)
                        both = jnp.where(
                            lanes_of((block, LANES)) < HD, acc[0, span], acc[1, span]
                        )
                        both = both + roll_lanes(both, HD)
                        there = (part, tile, which, pl.ds(rb * block, block))
                        mine = lanes_of((block, LANES)) // HD == lax.rem(group, 2)
                        dkv[there] = jnp.where(mine, both.astype(BF16), dkv[there])
            return 0

        lax.fori_loop(lo, hi, body, 0)
        clock[0] = start + (hi - lo) * 2 * per_rb

    for tile in range(KV // 2):
        attention(2 * tile, 2 * tile + 2, 1)
        for step in range(1, ctx_n):
            dkv_copy(lax.rem(ctx + step, ctx_n), tile, step - 1).start()
        if tile == 0:
            ysum.launch(False)

    ticks(2)
    def put_blocks(value, first):
        for j in range(value.shape[1] // LANES):
            at = first + j
            az[at // 2, pl.ds((at % 2) * shard, shard)] = value[:, j * LANES : (j + 1) * LANES]

    key_cols = KV * HD
    put_blocks(ysum.finish().astype(BF16), (width + 2 * key_cols) // LANES)

    for step in range(1, ctx_n):
        for tile in range(KV // 2):
            dkv_copy(lax.rem(ctx + step, ctx_n), tile, step - 1).wait_send()
            sender = lax.rem(ctx - step + ctx_n, ctx_n)
            pltpu.make_async_remote_copy(
                src_ref=dkv.at[sender, tile],
                dst_ref=dkv_in.at[sender, tile],
                send_sem=dkv_send.at[step - 1, tile],
                recv_sem=dkv_recv.at[step - 1, tile],
                device_id={"ctx": sender},
                device_id_type=MESH,
            ).wait_recv()
    cosine, sine = turn_ref[0], turn_ref[1]
    for tile in range(KV // 2):
        for which in range(2):
            part = dkv[ctx, tile, which].astype(F32)
            for step in range(1, ctx_n):
                part = part + dkv_in[lax.rem(ctx + step, ctx_n), tile, which].astype(F32)
            if which == 0:
                part = part * cosine - turned(part) * sine
            at = width + which * key_cols + tile * LANES
            gqkv[:, at : at + LANES] = part.astype(BF16)

    def query_partial(f):
        return across(a1_ref[:, pl.ds(pl.multiple_of(f * shard, shard), shard)], gqkv[...])

    xsum = RingSum(
        ring, query_partial, (xstage, xpair, xleft, xright), (xs0, xs1, xs2, xs3, xs4, xs5)
    )
    xsum.pair_all()
    xsum.launch(True)
    ticks(4)
    xsum.launch(False)
    ticks(4)

    def weight_copy(f):
        return pltpu.make_async_copy(wqkv_ref.at[f], wbuf.at[f % 2], wsem.at[f % 2])

    weight_copy(0).start()
    parts = []
    for f in range(fsdp_n):
        if f + 1 < fsdp_n:
            weight_copy(f + 1).start()
        weight_copy(f).wait()
        parts.append(through(gqkv[...], wbuf[f % 2]))
    da1 = jnp.concatenate(parts, 1)
    x = x_ref[...].astype(F32)
    factor = lax.rsqrt(jnp.mean(x * x, -1, keepdims=True) + EPSILON)
    unit = x * factor
    gain = gain_ref[...]
    gtok_ref[...] = (dh1_ref[...] + normed_back(unit, factor, da1, gain)).astype(BF16)
    mine = jnp.sum(da1 * unit, 0, keepdims=True)
    first_row = lax.broadcasted_iota(jnp.int32, (2, width), 0) == 0
    gslot[fsdp] = jnp.where(first_row, mine, gpart_ref[...])

    def gain_copy(slots, axis, here, step, sems):
        n = fsdp_n if axis == "fsdp" else ctx_n
        return pltpu.make_async_remote_copy(
            src_ref=slots.at[here],
            dst_ref=slots.at[here],
            send_sem=sems[0].at[step - 1],
            recv_sem=sems[1].at[step - 1],
            device_id={axis: lax.rem((fsdp if axis == "fsdp" else ctx) + step, n)},
            device_id_type=MESH,
        )

    def exchange(slots, axis, n, me, sems):
        for step in range(1, n):
            gain_copy(slots, axis, me, step, sems).start()
        for step in range(1, n):
            gain_copy(slots, axis, me, step, sems).wait_send()
            gain_copy(slots, axis, lax.rem(me - step + n, n), step, sems).wait_recv()
        total = slots[0]
        for i in range(1, n):
            total = total + slots[i]
        return total

    cslot[ctx] = exchange(gslot, "fsdp", fsdp_n, fsdp, (gain_send, gain_recv))
    gains_ref[...] = exchange(cslot, "ctx", ctx_n, ctx, (cgain_send, cgain_recv))

    put_blocks(xsum.finish().astype(BF16), 0)
    ticks(line.ticks - clock[0])


def back(gz, wqkv, q, o, do, dhb, a1, k_all, v_all, lse, mask, turn, x, dh1, gain, gpart):
    ctx_n = lax.axis_size("ctx")
    fsdp_n = lax.axis_size("fsdp")
    count, width = q.shape
    total = k_all.shape[0]
    local = gz.shape[1]
    shard = wqkv.shape[1]
    cols = wqkv.shape[2]
    chips = fsdp_n // 2
    far = chips // 2
    vmem = pl.BlockSpec(memory_space=pltpu.VMEM)
    hbm = pl.BlockSpec(memory_space=pl.ANY)
    dma = pltpu.SemaphoreType.DMA
    zbuf = pltpu.VMEM((SLOTS, local, LANES), BF16)

    def ring_bufs(wide):
        return [
            pltpu.VMEM((2, shard, wide), BF16),
            pltpu.VMEM((chips, shard, wide), BF16),
            pltpu.VMEM((far, shard, wide), BF16),
            pltpu.VMEM((far, shard, wide), BF16),
        ]

    ring_sems = [
        dma((chips,)),
        dma((chips,)),
        dma((far, 2)),
        dma((far, 2)),
        dma((far, 2)),
        dma((far, 2)),
    ]
    blocks = (cols + width) // LANES
    scratch = (
        [zbuf] * 5
        + [pltpu.VMEM((SLOTS, LANES, local), BF16)]
        + [pltpu.VMEM((blocks // 2, 2 * shard, LANES), BF16)]
        + ring_bufs(cols)
        + ring_bufs(width)
        + [
            pltpu.VMEM((2, total, LANES), BF16),
            pltpu.VMEM((2, total, LANES), BF16),
            pltpu.VMEM((2, total, LANES), F32),
            pltpu.VMEM((2, total, LANES), F32),
            pltpu.VMEM((ctx_n, KV // 2, 2, count, LANES), BF16),
            pltpu.VMEM((ctx_n, KV // 2, 2, count, LANES), BF16),
            pltpu.VMEM((count, cols), BF16),
            pltpu.VMEM((2, shard, cols), BF16),
            pltpu.VMEM((fsdp_n, 2, width), F32),
            pltpu.VMEM((ctx_n, 2, width), F32),
        ]
        + [
            dma((SLOTS,)),
            dma((SLOTS,)),
            dma((SLOTS,)),
            dma((SLOTS,)),
            dma((SLOTS,)),
            dma((SLOTS, 2)),
            pltpu.SemaphoreType.REGULAR,
            pltpu.SemaphoreType.REGULAR,
        ]
        + ring_sems
        + ring_sems
        + [
            dma((ctx_n - 1, KV // 2)),
            dma((ctx_n - 1, KV // 2)),
            dma((fsdp_n - 1,)),
            dma((fsdp_n - 1,)),
            dma((ctx_n - 1,)),
            dma((ctx_n - 1,)),
            dma((2,)),
        ]
    )
    return pl.pallas_call(
        functools.partial(back_kernel, (ctx_n, fsdp_n)),
        out_shape=(
            jax.ShapeDtypeStruct((count, width), BF16),
            jax.ShapeDtypeStruct((2, width), F32),
            jax.ShapeDtypeStruct((width, local), BF16),
            jax.ShapeDtypeStruct((width, local), BF16),
            jax.ShapeDtypeStruct((local, width), BF16),
            jax.ShapeDtypeStruct((shard, cols), BF16),
            jax.ShapeDtypeStruct((shard, width), BF16),
        ),
        in_specs=[hbm, hbm] + [vmem] * 14,
        out_specs=(vmem, vmem, hbm, hbm, hbm, hbm, hbm),
        scratch_shapes=scratch,
        compiler_params=pltpu.CompilerParams(
            collective_id=1, has_side_effects=True, vmem_limit_bytes=VMEM_LIMIT
        ),
        name="back",
    )(gz, wqkv, q, o, do, dhb, a1, k_all, v_all, lse, mask, turn, x, dh1, gain, gpart)


def shards(
    tokens,
    cotangent,
    block_table,
    gain_attn,
    w_query,
    w_key,
    w_value,
    w_output,
    gain_mlp,
    w_gate,
    w_up,
    w_down,
):
    ctx_n = lax.axis_size("ctx")
    ctx = lax.axis_index("ctx")
    count, width = tokens.shape[1:]
    block = count // 2
    local = w_gate.shape[1]

    table = block_table.reshape(ctx_n, 2)
    lower, upper = jnp.min(table, 1), jnp.max(table, 1)
    owned = table[ctx]
    swap = owned[0] > owned[1]

    def ordered(rows):
        return jnp.where(swap, jnp.concatenate([rows[block:], rows[:block]], 0), rows)

    offsets = jnp.arange(block, dtype=jnp.int32)
    spots = jnp.stack([lower, upper])[:, :, None] * block + offsets
    own_spots = spots[:, ctx]
    key_spots = spots.reshape(2, -1)
    mask = jnp.where(own_spots[:, :, None] >= key_spots[:, None, :], 0.0, NEGATIVE).astype(F32)
    freqs = 10000.0 ** (-jnp.arange(HD // 2, dtype=F32) / (HD // 2))
    angle = own_spots.reshape(-1).astype(F32)[:, None] * freqs[None, :]
    angle = jnp.concatenate([angle] * (LANES * 2 // HD), -1)
    turn = jnp.stack([jnp.cos(angle), jnp.sin(angle)])

    rows_in = ordered(tokens[0])
    grad_out = ordered(cotangent[0])

    wqkv = lax.all_gather(jnp.concatenate([w_query, w_key, w_value], 1), "fsdp", axis=0)
    full_output = lax.all_gather(w_output, "fsdp", axis=0)
    inputs = rows_in.astype(F32)
    unit_one, factor_one, normal_one = normed(inputs, gain_attn)
    qkv = matmul(normal_one, wqkv.reshape(width, -1))

    def rotary(values):
        heads = values.reshape(count, -1, HD)
        middle = HD // 2
        spun = jnp.concatenate([-heads[..., middle:], heads[..., :middle]], -1)
        cosine, sine = turn[:, :, None, :HD]
        return (heads * cosine + spun * sine).reshape(count, -1).astype(BF16)

    key_cols = KV * HD
    queries = rotary(qkv[:, :width])
    keys_own = rotary(qkv[:, width : width + key_cols])
    values_own = qkv[:, width + key_cols :].astype(BF16)

    def gathered(rows):
        every = lax.all_gather(rows, "ctx", axis=0).reshape(ctx_n, 2, block, key_cols)
        return every.transpose(1, 0, 2, 3).reshape(-1, key_cols)

    keys_all, values_all = gathered(keys_own), gathered(values_own)
    mixed, lse = attend(queries, keys_all, values_all, mask)
    attn_out = lax.dot_general(
        mixed, full_output, (((1,), (1,)), ((), ())), preferred_element_type=F32
    ).reshape(count, width)
    hidden_one = inputs + attn_out
    unit_two, factor_two, normal_two = normed(hidden_one, gain_mlp)
    rows_all = lax.all_gather(normal_two, "fsdp", axis=0, tiled=True)
    grad_all = lax.all_gather(grad_out, "fsdp", axis=0, tiled=True)
    gate = matmul(rows_all, w_gate)
    up = matmul(rows_all, w_up)
    grad_hidden = through(grad_all, w_down)
    hidden, grad_gate_in, grad_up_in = gate_back(grad_hidden, gate, up)

    def scattered(partial):
        return lax.psum_scatter(
            partial.astype(BF16), "fsdp", scatter_dimension=0, tiled=True
        ).astype(F32)

    grad_normal_two = scattered(through(grad_gate_in, w_gate) + through(grad_up_in, w_up))
    mlp_out = scattered(matmul(hidden, w_down))

    def chunks(partial):
        return partial.astype(BF16).reshape(local, -1, LANES).transpose(1, 0, 2)

    gz = jnp.concatenate(
        [
            chunks(across(grad_gate_in, rows_all)),
            chunks(across(grad_up_in, rows_all)),
            chunks(across(hidden, grad_all)),
        ],
        0,
    )
    result = (hidden_one + mlp_out).astype(BF16)
    grad_hidden_one = grad_out.astype(F32) + normed_back(
        unit_two, factor_two, grad_normal_two, gain_mlp
    )
    grad_mixed_in = grad_hidden_one.astype(BF16)
    shard = w_output.shape[1]
    split = grad_mixed_in.reshape(count, -1, shard)
    grad_mixed = lax.dot_general(
        split, full_output, (((1, 2), (0, 2)), ((), ())), preferred_element_type=F32
    ).astype(BF16)
    gpart = jnp.sum(grad_normal_two * unit_two, 0, keepdims=True)
    grad_tokens, gains, gate_sum, up_sum, down_sum, query_sum, output_sum = back(
        gz,
        wqkv,
        queries,
        mixed,
        grad_mixed,
        grad_mixed_in,
        normal_one,
        keys_all,
        values_all,
        lse,
        mask,
        turn,
        rows_in,
        grad_hidden_one,
        gain_attn[None],
        gpart,
    )
    query_sum = query_sum.astype(F32)
    return (
        ordered(result)[None],
        ordered(grad_tokens)[None],
        query_sum[:, :width],
        query_sum[:, width : width + key_cols],
        query_sum[:, width + key_cols :],
        output_sum.T.astype(F32),
        gate_sum.astype(F32),
        up_sum.astype(F32),
        down_sum.astype(F32),
        gains[0],
        gains[1],
    )


def solution(mesh):
    in_specs = (
        P("fsdp", "ctx", None),
        P("fsdp", "ctx", None),
        P(),
        P(),
        P("fsdp", None),
        P("fsdp", None),
        P("fsdp", None),
        P(None, "fsdp"),
        P(),
        P(None, "fsdp"),
        P(None, "fsdp"),
        P("fsdp", None),
    )
    out_specs = (
        P("fsdp", "ctx", None),
        P("fsdp", "ctx", None),
        P("fsdp", None),
        P("fsdp", None),
        P("fsdp", None),
        P(None, "fsdp"),
        P(None, "fsdp"),
        P(None, "fsdp"),
        P("fsdp", None),
        P(),
        P(),
    )
    return jax.shard_map(shards, mesh=mesh, in_specs=in_specs, out_specs=out_specs, check_vma=False)
```

time: 1140 us -> 811 us (0.71)
  waiting for transfers between devices: 729 us -> 203 us
  Pallas kernels: 0 us -> 331 us
  matrix products: 211 us -> 119 us
  blocking collectives: 78.3 us -> 32.3 us
  local copies, waits for them, and re-layouts: 36.6 us -> 60 us
  other arithmetic: 66.7 us -> 43.4 us
    pallas_call x0 -> x2, Pallas kernels: none -> 331 us  [the longest x1 316 us: back(): pl.pallas_call(functools.partial(back_kernel, (ctx_n, fsdp_n)), out_shape...]
    psum x1 -> x0, waiting for transfers between devices: 318 us -> none  [shards(): lax.psum(part.astype(jnp.bfloat16), 'ctx').astype(jnp.float32)]
    reduce_scatter x5 -> x2, waiting for transfers between devices: 249 us -> 95.5 us  [scattered(): lax.psum_scatter(partial.astype(BF16), 'fsdp', scatter_dimension=0, tiled...]
    dot_general x49 -> x12, matrix products: 211 us -> 119 us  [the longest x10 104 us: dot(): lax.dot_general(left, right, (((left_dim,), (right_dim,)), ((), ())), pre...]
    psum x1 -> x0, blocking collectives: 46.1 us -> none  [shards(): lax.psum((jnp.sum(grad_normal_one * unit_one, 0), jnp.sum(grad_normal_two...]
    all_gather x4 -> x2, waiting for transfers between devices: 67.8 us -> 40 us  [the longest x1 40 us: shards(): lax.all_gather(jnp.concatenate([w_query, w_key, w_value], 1), 'fsdp', axi...]
    slice x2 -> x13, local copies, waits for them, and re-layouts: 2.53 us -> 18.7 us  [the longest x4 5.72 us: ordered(): rows[block:]]
    all_gather x1, waiting for transfers between devices: 37 us -> 21.3 us  [shards(): grad_all = lax.all_gather(grad_out, 'fsdp', axis=0, tiled=True)]
  transfers between devices with their start and end apart: 12 -> 6, of which waited for: 12 -> 5; matrix products, arithmetic and copies ran while one was open for 14% -> 16% of each run, Pallas kernels for 0% -> 2%
where the time goes in v2:
time: 811 us; the launch traced here: 806 us
  Pallas kernels  331 us (41%)
  waiting for transfers between devices  203 us (25%)
  matrix products  119 us (15%)
  local copies, waits for them, and re-layouts  60 us (7%)
  other arithmetic  43.4 us (5%)
  blocking collectives  32.3 us (4%)
  between operations  16 us (2%)
    pallas_call x1, Pallas kernels, back(): pl.pallas_call(functools.partial(back_kernel, (ctx_n, fsdp_n)), out_shape...  316 us
    dot_general x10, matrix products, dot(): lax.dot_general(left, right, (((left_dim,), (right_dim,)), ((), ())), pre...  104 us
    reduce_scatter x2, waiting for transfers between devices, scattered(): lax.psum_scatter(partial.astype(BF16), 'fsdp', scatter_dimension=0, tiled...  95.5 us
    all_gather x1, waiting for transfers between devices, shards(): rows_all = lax.all_gather(normal_two, 'fsdp', axis=0, tiled=True)  45.7 us
    all_gather x1, waiting for transfers between devices, shards(): lax.all_gather(jnp.concatenate([w_query, w_key, w_value], 1), 'fsdp', axi...  40 us
    all_gather x2, blocking collectives, gathered(): lax.all_gather(rows, 'ctx', axis=0).reshape(ctx_n, 2, block, key_cols)  32.3 us
    all_gather x1, waiting for transfers between devices, shards(): grad_all = lax.all_gather(grad_out, 'fsdp', axis=0, tiled=True)  21.3 us
    unnamed x75, local copies, waits for them, and re-layouts  19.8 us
  transfers between devices with their start and end apart: 6, of which 5 were waited for; matrix products, arithmetic and copies ran while one was open for 16% of the time, Pallas kernels for 2%

profile of v2, /device:TPU:0, one launch (start us, length us, event | category | flops | bytes accessed | tf_op | source)
XLA Modules:
  0.0 805.8 jit_solution(15372817386007631696)
XLA Ops:
  7.3 2.7 pad_maximum_fusion.1
  14.0 2.6 maximum_select_fusion.5
  19.4 2.3 copy.50
  23.3 2.9 copy.35
  26.2 2.5 slice_bitcast_fusion.5
  28.6 2.1 copy.61
  30.7 2.1 copy.60
  32.7 2.7 fusion.8
  36.5 40.0 %all-gather.13.cloned.1.call-done = bf16[2048,2560]{1,0:T(8,128)(2,1)} async-done(((bf16[256,2560]{1,0:T(8,128)(2,1)}), bf16[2048,2560]{1,0:T(8,128)(2,1)}) %all-gather.13.cloned.1.call-update) | async-done | bytes 10485776 | tf_op jit(solution)/shard_map/all_gather | solution.py:957
  76.5 6.2 fusion.15
  87.0 1.6 maximum_multiply_fusion.1
  90.7 16.0 %all-gather.1 = bf16[1024,256]{1,0:T(8,128)(2,1)S(1)} all-gather(bf16[256,256]{1,0:T(8,128)(2,1)S(1)} %add_convert_fusion.3), channel_id=3, replica_groups=mesh['ctx'=4,'fsdp'=8] {'ctx'}, dimensions={0}, use_global_device_ids=true | all-gather | bytes 655360 | tf_op jit(solution)/shard_map/all_gather | solution.py:976
  107.5 16.3 %all-gather.2 = bf16[1024,256]{1,0:T(8,128)(2,1)S(1)} all-gather(bf16[256,256]{1,0:T(8,128)(2,1)} %slice.136), channel_id=4, replica_groups=mesh['ctx'=4,'fsdp'=8] {'ctx'}, dimensions={0}, use_global_device_ids=true | all-gather | bytes 655360 | tf_op jit(solution)/shard_map/all_gather | solution.py:976
  124.7 2.9 copy.36
  127.6 1.8 slice_negate_fusion
  130.9 3.0 copy.38
  133.9 4.3 add_convert_fusion.2.q_ref
  138.2 15.2 %attend.1 = (bf16[256,2048]{1,0:T(8,128)(2,1)}, f32[2,512,128]{2,1,0:T(8,128)}) custom-call(bf16[256,2048]{1,0:T(8,128)(2,1)} %add_convert_fusion.2.q_ref, bf16[1024,256]{1,0:T(8,128)(2,1)} %bitcast.129, bf16[1024,256]{1,0:T(8,128)(2,1)} %bitcast.131, f32[2,128,512]{2,1,0:T(8,128)} %compare_select_fusion.mask_ref), custom_call_target="tpu_custom_call" | custom-call | flops 2147483648 | bytes 4194304 | tf_op jit(solution)/shard_map/attend/pallas_call | solution.py:138
  153.4 8.5 %multiply_reduce_fusion = (f32[256]{0:T(256)S(1)}, f32[256,8,256]{0,2,1:T(8,128)}) fusion(bf16[256,8,256]{0,2,1:T(8,128)(2,1)} %bitcast.137, bf16[128,8,256]{0,2,1:T(8,128)(2,1)S(1)} %bitcast.140, bf16[128,8,256]{0,2,1:T(8,128)(2,1)} %bitcast.141, pred[]{:T(512)} %bitcast, bf16[8,2048,256]{2,1,0:T(8,128)(2,1)} %bitcast.150, ...), kind=kOutput, calls=%fused_computation.34 | convolution fusion | flops 2152201984 | bytes 13632513 | tf_op jit(solution)/shard_map/dot_general | solution.py:981
  161.9 3.1 copy.59
  164.9 3.2 multiply_convert_fusion.3
  168.4 21.3 %all-gather.11.cloned.1.call-done = bf16[2048,2048]{1,0:T(8,128)(2,1)} async-done(((bf16[256,2048]{1,0:T(8,128)(2,1)}), bf16[2048,2048]{1,0:T(8,128)(2,1)}) %all-gather.11.cloned.1.call-update) | async-done | bytes 8388624 | tf_op jit(solution)/shard_map/all_gather | solution.py:987
  189.7 11.0 %fusion.41 = f32[2048,704]{0,1:T(8,128)} fusion(bf16[2048,2048]{1,0:T(8,128)(2,1)} %all-gather.11.cloned.1.call-done, bf16[704,2048]{1,0:T(8,128)(2,1)} %param.23), kind=kOutput, calls=%fused_computation.98 | convolution fusion | flops 5905580032 | bytes 17039360 | tf_op jit(solution)/shard_map/dot_general | solution.py:27
  200.7 45.7 %all-gather.9.cloned.1.call-done = bf16[2048,2048]{1,0:T(8,128)(2,1)} async-done(((bf16[256,2048]{1,0:T(8,128)(2,1)}), bf16[2048,2048]{1,0:T(8,128)(2,1)}) %all-gather.9.cloned.1.call-update) | async-done | bytes 8388624 | tf_op jit(solution)/shard_map/all_gather | solution.py:986
  246.4 11.2 %fusion.40 = f32[2048,704]{0,1:T(8,128)} fusion(bf16[2048,2048]{1,0:T(8,128)(2,1)} %all-gather.9.cloned.1.call-done, bf16[2048,704]{0,1:T(8,128)(2,1)} %param.22), kind=kOutput, calls=%fused_computation.97 | convolution fusion | flops 5905580032 | bytes 17039360 | tf_op jit(solution)/shard_map/dot_general | solution.py:27
  257.6 12.9 %multiply_convert_fusion.1 = (bf16[2048,704]{0,1:T(8,128)(2,1)}, bf16[2048,704]{0,1:T(8,128)(2,1)}, bf16[2048,704]{0,1:T(8,128)(2,1)}) fusion(f32[2048,704]{0,1:T(8,128)S(1)} %copy-done.29, f32[2048,704]{0,1:T(8,128)} %fusion.40, bf16[2048,2048]{1,0:T(8,128)(2,1)S(1)} %copy-done.26, bf16[2048,704]{0,1:T(8,128)(2,1)S(1)} %copy-done), kind=kOutput, calls=%fused_computation.4 | convolution fusion | flops 5927206912 | bytes 31457280 | tf_op jit(solution)/shard_map/dot_general | solution.py:27
  270.5 12.9 %fusion.42 = f32[2048,2048]{1,0:T(8,128)} fusion(bf16[2048,704]{0,1:T(8,128)(2,1)} %get-tuple-element.59, bf16[2048,704]{0,1:T(8,128)(2,1)S(1)} %copy-done), kind=kOutput, calls=%fused_computation.99 | convolution fusion | flops 5905580032 | bytes 22544384 | tf_op jit(solution)/shard_map/dot_general | solution.py:27
  283.4 12.5 %add_convert_fusion = bf16[2048,2048]{1,0:T(8,128)(2,1)} fusion(f32[2048,2048]{1,0:T(8,128)} %fusion.42, bf16[2048,704]{0,1:T(8,128)(2,1)S(1)} %copy-done.31, bf16[2048,704]{0,1:T(8,128)(2,1)S(1)} %copy-done.27), kind=kOutput, calls=%fused_computation | convolution fusion | flops 5913968640 | bytes 30932992 | tf_op jit(solution)/shard_map/dot_general | solution.py:27
  296.0 1.7 copy-done.28
  297.7 11.2 %convolution_convert_fusion = bf16[2048,2048]{1,0:T(8,128)(2,1)} fusion(bf16[2048,704]{0,1:T(8,128)(2,1)} %get-tuple-element.61, bf16[704,2048]{1,0:T(8,128)(2,1)S(1)} %copy-done.28), kind=kOutput, calls=%fused_computation.2 | convolution fusion | flops 5909774336 | bytes 14155776 | tf_op jit(solution)/shard_map/dot_general | solution.py:27
  310.6 9.9 %fusion.13 = bf16[88,16,8,128]{3,2,1,0:T(8,128)(2,1)S(1)} fusion(bf16[2048,704]{0,1:T(8,128)(2,1)} %get-tuple-element.61, bf16[2048,2048]{1,0:T(8,128)(2,1)} %all-gather.11.cloned.1.call-done), kind=kOutput, calls=%fused_computation.39 | convolution fusion | flops 5907021824 | bytes 14155776 | tf_op jit(solution)/shard_map/dot_general | solution.py:27
  321.3 9.4 %fusion.12 = bf16[88,16,8,128]{3,2,1,0:T(8,128)(2,1)S(1)} fusion(bf16[2048,704]{0,1:T(8,128)(2,1)S(1)} %copy-done.32, bf16[2048,2048]{1,0:T(8,128)(2,1)} %all-gather.9.cloned.1.call-done), kind=kOutput, calls=%fused_computation.38 | convolution fusion | flops 5907021824 | bytes 14155776 | tf_op jit(solution)/shard_map/dot_general | solution.py:27
  332.6 6.3 fusion.11
  339.7 4.2 pad_maximum_fusion.gz_ref
  343.9 23.5 %reduce-scatter.5.cloned.1.call-done = bf16[256,2048]{1,0:T(8,128)(2,1)} async-done(((bf16[2048,2048]{1,0:T(8,128)(2,1)}), bf16[256,2048]{1,0:T(8,128)(2,1)}) %reduce-scatter.5.cloned.1.call-update) | async-done | bytes 1048592 | tf_op jit(solution)/shard_map/reduce_scatter | solution.py:994
  367.4 3.0 fusion.7
  370.4 72.0 %reduce-scatter.3.cloned.1.call-done = bf16[256,2048]{1,0:T(8,128)(2,1)} async-done(((bf16[2048,2048]{1,0:T(8,128)(2,1)}), bf16[256,2048]{1,0:T(8,128)(2,1)}) %reduce-scatter.3.cloned.1.call-update) | async-done | bytes 1048592 | tf_op jit(solution)/shard_map/reduce_scatter | solution.py:994
  442.4 5.2 fusion.33
  447.6 7.1 fusion.1.do_ref
  454.7 316.0 %back.1 = (bf16[256,2048]{1,0:T(8,128)(2,1)}, f32[2,2048]{1,0:T(2,128)}, bf16[2048,704]{1,0:T(8,128)(2,1)}, bf16[2048,704]{1,0:T(8,128)(2,1)}, bf16[704,2048]{1,...) custom-call(bf16[48,704,128]{2,1,0:T(8,128)(2,1)} %pad_maximum_fusion.gz_ref, ...), custom_call_target="tpu_custom_call" | custom-call | tf_op jit(solution)/shard_map/back/pallas_call | solution.py:895
  770.7 1.9 fusion.35
  772.6 2.8 slice.124
  776.0 1.6 convert_bitcast_fusion
  777.6 3.0 copy.55
  782.6 5.2 copy.56
  787.8 5.4 copy.57
  793.2 3.3 convert_element_type.126
  796.6 2.2 fusion.21
  (125 shorter events, 25.6 us)
Async XLA Ops:
  7.2 250.4 %copy-start = (bf16[2048,704]{0,1:T(8,128)(2,1)S(1)}, bf16[2048,704]{0,1:T(8,128)(2,1)}, u32[]{:S(2)}) copy-start(bf16[2048,704]{0,1:T(8,128)(2,1)} %param.21) | copy-start | bytes 8650756
  7.2 3.5 copy-start.25
  7.2 69.3 %all-gather.13.cloned.1.call-start = ((), (), s32[]{:S(2)}) async-start(), calls=%async_computation.6 | async-start | bytes 11796480 | tf_op jit(solution)/shard_map/all_gather | solution.py:957
  9.9 143.5 %all-gather.15.cloned.1.call-start = ((), (), s32[]{:S(2)}) async-start(), calls=%async_computation.7 | async-start | bytes 9437184 | tf_op jit(solution)/shard_map/all_gather | solution.py:958
  10.7 179.0 %all-gather.11.cloned.1.call-start = ((), (), s32[]{:S(2)}) async-start(), calls=%async_computation.4 | async-start | bytes 9437184 | tf_op jit(solution)/shard_map/all_gather | solution.py:987
  16.6 229.8 %all-gather.9.cloned.1.call-start = ((), (), s32[]{:S(2)}) async-start(), calls=%async_computation.2 | async-start | bytes 9437184 | tf_op jit(solution)/shard_map/all_gather | solution.py:986
  17.7 5.6 copy-start.13
  28.6 47.9 %copy-start.20 = (f32[2048]{0:T(1024)S(1)}, f32[2048]{0:T(1024)}, u32[]{:S(2)}) copy-start(f32[2048]{0:T(1024)} %param.15) | copy-start | bytes 24580
  35.4 47.3 %copy-start.23 = (f32[256]{0:T(256)}, f32[256]{0:T(256)S(1)}, u32[]{:S(2)}) copy-start(f32[256]{0:T(256)S(1)} %add_rsqrt_fusion.1) | copy-start | bytes 3076
  82.7 1.6 copy-start.5
  84.4 5.3 copy-start.16
  127.6 1.8 copy-start.17
  138.2 15.2 %copy-start.18 = (bf16[1,128,2048]{1,2,0:T(8,128)(2,1)S(1)}, bf16[1,128,2048]{1,2,0:T(8,128)(2,1)}, u32[]{:S(2)}) copy-start(bf16[1,128,2048]{1,2,0:T(8,128)(2,1)} %copy.61) | copy-start | bytes 1572868
  161.9 3.1 copy-start.19
  168.1 199.3 %reduce-scatter.5.cloned.1.call-start = ((), (), s32[]{:S(2)}) async-start(), calls=%async_computation.5 | async-start | bytes 9437184 | tf_op jit(solution)/shard_map/reduce_scatter | solution.py:994
  246.4 11.2 %copy-start.26 = (bf16[2048,2048]{1,0:T(8,128)(2,1)S(1)}, bf16[2048,2048]{1,0:T(8,128)(2,1)}, u32[]{:S(2)}) copy-start(bf16[2048,2048]{1,0:T(8,128)(2,1)} %all-gather.9.cloned.1.call-done) | copy-start | bytes 25165828
  246.4 11.2 %copy-start.29 = (f32[2048,704]{0,1:T(8,128)S(1)}, f32[2048,704]{0,1:T(8,128)}, u32[]{:S(2)}) copy-start(f32[2048,704]{0,1:T(8,128)} %fusion.41) | copy-start | bytes 17301508
  270.5 12.9 %copy-start.27 = (bf16[2048,704]{0,1:T(8,128)(2,1)S(1)}, bf16[2048,704]{0,1:T(8,128)(2,1)}, u32[]{:S(2)}) copy-start(bf16[2048,704]{0,1:T(8,128)(2,1)} %param.22) | copy-start | bytes 8650756
  270.5 12.9 %copy-start.31 = (bf16[2048,704]{0,1:T(8,128)(2,1)S(1)}, bf16[2048,704]{0,1:T(8,128)(2,1)}, u32[]{:S(2)}) copy-start(bf16[2048,704]{0,1:T(8,128)(2,1)} %get-tuple-element.60) | copy-start | bytes 8650756
  295.9 1.8 copy-start.28
  295.9 146.5 %reduce-scatter.3.cloned.1.call-start = ((), (), s32[]{:S(2)}) async-start(), calls=%async_computation.3 | async-start | bytes 9437184 | tf_op jit(solution)/shard_map/reduce_scatter | solution.py:994
  308.9 0.9 copy-start.14
  310.6 10.7 %copy-start.32 = (bf16[2048,704]{0,1:T(8,128)(2,1)S(1)}, bf16[2048,704]{0,1:T(8,128)(2,1)}, u32[]{:S(2)}) copy-start(bf16[2048,704]{0,1:T(8,128)(2,1)} %get-tuple-element.60) | copy-start | bytes 8650756
  320.5 11.0 %slice-start = ((s8[8388608]{0:T(1024)(128)(4,1)}), s8[4194304]{0:T(1024)(128)(4,1)S(1)}, s32[]{:S(2)}) async-start(s8[8388608]{0:T(1024)(128)(4,1)} %bitcast.152), calls=%async_computation.8 | async-start | bytes 8388608
  321.3 10.2 %slice-start.1 = ((s8[8388608]{0:T(1024)(128)(4,1)}), s8[4194304]{0:T(1024)(128)(4,1)S(1)}, s32[]{:S(2)}) async-start(s8[8388608]{0:T(1024)(128)(4,1)} %bitcast.152), calls=%async_computation.9 | async-start | bytes 8388608
  330.8 1.8 copy-start.30
  339.6 27.7 %copy-start.2 = (f32[256,2048]{1,0:T(8,128)S(1)}, f32[256,2048]{1,0:T(8,128)}, u32[]{:S(2)}) copy-start(f32[256,2048]{1,0:T(8,128)} %copy.59) | copy-start | bytes 6291460
  343.8 98.6 %copy-start.21 = (f32[2048]{0:T(1024)S(1)}, f32[2048]{0:T(1024)}, u32[]{:S(2)}) copy-start(f32[2048]{0:T(1024)} %param.15) | copy-start | bytes 24580
  343.9 98.6 %copy-start.24 = (f32[256]{0:T(256)S(1)}, f32[256]{0:T(256)}, u32[]{:S(2)}) copy-start(f32[256]{0:T(256)} %copy-done.23) | copy-start | bytes 3076
  447.6 7.1 copy-start.6
  770.7 4.7 copy-start.22
  770.7 5.3 copy-start.15
  777.6 3.0 copy-start.7
  777.6 3.9 copy-start.3
  787.8 5.4 copy-start.9
  793.2 3.4 copy-start.4
  793.2 3.4 copy-start.8
  793.2 3.4 copy-start.10
  793.2 3.3 copy-start.11
  793.2 3.3 copy-start.12
  796.6 2.2 copy-start.1
Sparse Core Ops, SparseCore 0:
  10.5 65.9 all-gather.12
  78.4 54.3 all-gather.14
  135.3 54.3 all-gather.10
  192.0 54.3 all-gather.8
  296.1 71.2 reduce-scatter.4
  371.1 71.2 reduce-scatter.2

commit v3 on v2

v3 whole, which is shorter than its diff:
```python
import functools

import jax
import jax.numpy as jnp
from jax import lax
from jax.experimental import pallas as pl
from jax.experimental.pallas import tpu as pltpu
from jax.sharding import PartitionSpec as P

H = 32
KV = 4
HD = 64
GROUP = H // KV
PAIRS = GROUP // 2
LANES = 128

EPSILON = 1e-05
NEGATIVE = -1e30
SLOTS = 6
VMEM_LIMIT = 60 * 1024 * 1024
MESH = pl.DeviceIdType.MESH
F32 = jnp.float32
BF16 = jnp.bfloat16


def dot(left, right, left_dim, right_dim):
    return lax.dot_general(
        left, right, (((left_dim,), (right_dim,)), ((), ())), preferred_element_type=F32
    )


def matmul(left, right):
    return dot(left, right, 1, 0)


def across(left, right):
    return dot(left, right, 0, 0)


def through(left, right):
    return dot(left, right, 1, 1)


def normed(hidden, gain):
    factor = lax.rsqrt(jnp.mean(hidden * hidden, -1, keepdims=True) + EPSILON)
    unit = hidden * factor
    return (unit, factor, (unit * gain).astype(BF16))


def normed_back(unit, factor, grad_in, gain):
    scaled = grad_in * gain
    return factor * (scaled - unit * jnp.mean(scaled * unit, -1, keepdims=True))


def gate_back(grad_hidden, gate, up):
    sigma = jax.nn.sigmoid(gate)
    activated = gate * sigma
    grad_gate_in = (grad_hidden * up * sigma * (1.0 + gate * (1.0 - sigma))).astype(BF16)
    grad_up_in = (grad_hidden * activated).astype(BF16)
    return ((activated * up).astype(BF16), grad_gate_in, grad_up_in)


def lanes_of(shape):
    return lax.broadcasted_iota(jnp.int32, shape, len(shape) - 1)


def roll_lanes(value, amount):
    return pltpu.roll(value, amount, 1)


def turned(value):
    first = lax.rem(lanes_of(value.shape), HD) < HD // 2
    return jnp.where(first, -roll_lanes(value, LANES - HD // 2), roll_lanes(value, HD // 2))


def stacked(ref, rows, group):
    wide = PAIRS * LANES
    block = ref[rows, pl.ds(pl.multiple_of(group * wide, wide), wide)]
    return jnp.concatenate([block[:, j * LANES : (j + 1) * LANES] for j in range(PAIRS)], 0)


def spread_heads(ref, out_ref, group):
    at = pl.multiple_of((group // 2) * LANES, LANES)
    tile = ref[:, pl.ds(at, LANES)].astype(F32)
    other = roll_lanes(tile, HD)
    half = lanes_of(tile.shape) // HD
    here = lax.rem(group, 2)
    for par in range(2):
        picked = jnp.where(here == par, tile, other)
        out_ref[par] = jnp.where(half == par, picked, 0.0).astype(BF16)


def attend_kernel(q_ref, k_ref, v_ref, mask_ref, o_ref, lse_ref, kz, vz):
    block = q_ref.shape[0] // 2
    keys = k_ref.shape[0] // 2
    scale = HD ** (-0.5)
    lse_ref[...] = jnp.zeros_like(lse_ref)

    def per_group(group, _):
        spread_heads(k_ref, kz, group)
        spread_heads(v_ref, vz, group)
        for rb in range(2):
            rows = pl.ds(rb * block, block)
            q4 = stacked(q_ref, rows, group) * jnp.asarray(scale, BF16)
            mask = mask_ref[rb]
            mask = jnp.concatenate([mask] * PAIRS, 0)
            total = 0.0
            lse = lse_ref[rb]
            for par in range(2):
                low = through(q4, kz[par, pl.ds(0, keys)])
                scores = [low + mask] if rb == 0 else [low]
                if rb == 1:
                    scores.append(through(q4, kz[par, pl.ds(keys, keys)]) + mask)
                peak = functools.reduce(
                    jnp.maximum, [jnp.max(s, -1, keepdims=True) for s in scores]
                )
                probs = [jnp.exp(s - peak) for s in scores]
                norm = sum(jnp.sum(p, -1, keepdims=True) for p in probs)
                mixed = sum(
                    matmul(p.astype(BF16), vz[par, pl.ds(i * keys, keys)])
                    for i, p in enumerate(probs)
                )
                total = total + mixed / norm
                lse = jnp.where(lanes_of(lse.shape) == 2 * group + par, peak + jnp.log(norm), lse)
            lse_ref[rb] = lse
            for j in range(PAIRS):
                at = pl.multiple_of((group * PAIRS + j) * LANES, LANES)
                o_ref[rows, pl.ds(at, LANES)] = total[j * block : (j + 1) * block].astype(BF16)
        return 0

    lax.fori_loop(0, KV, per_group, 0)


def attend(q, k_all, v_all, mask):
    count = q.shape[0]
    total = k_all.shape[0]
    vmem = pl.BlockSpec(memory_space=pltpu.VMEM)
    return pl.pallas_call(
        attend_kernel,
        out_shape=(
            jax.ShapeDtypeStruct((count, H * HD), BF16),
            jax.ShapeDtypeStruct((2, PAIRS * count // 2, LANES), F32),
        ),
        in_specs=[vmem] * 4,
        out_specs=(vmem, vmem),
        scratch_shapes=[
            pltpu.VMEM((2, total, LANES), BF16),
            pltpu.VMEM((2, total, LANES), BF16),
        ],
        compiler_params=pltpu.CompilerParams(vmem_limit_bytes=VMEM_LIMIT),
        cost_estimate=pl.CostEstimate(
            flops=4 * count * total * H * HD, bytes_accessed=4 << 20, transcendentals=H * count * total
        ),
        name="attend",
    )(q, k_all, v_all, mask)


class LineSum:
    def __init__(self, count, index, first, second, sources, targets, bufs, sems):
        self.n = count
        self.first, self.second = first, second
        self.total = first + second
        self.mlp_src, self.att_src = sources
        self.gate_dst, self.up_dst, self.down_dst, self.query_dst, self.output_dst = targets
        self.own, self.rout, self.sums, self.rin, self.done = bufs
        (
            self.load_sem,
            self.in_send,
            self.rout_sem,
            self.rin_sem,
            self.out_send,
            self.store_sem,
            self.credit_in,
            self.credit_out,
        ) = sems
        half = count // 2
        left = index < half
        self.depth = jnp.where(left, index, count - 1 - index)
        step = jnp.where(left, 1, -1)
        self.inward = index + step
        outward = index - step
        self.has_out = self.depth > 0
        self.outward = jnp.where(self.has_out, outward, index + step)
        self.is_mid = self.depth == half - 1
        deepest = half - 1
        self.lag_sum = 1 + 2 * self.depth
        self.lag_sent = self.lag_sum + 2
        self.lag_total = 1 + 2 * deepest + 2 + 2 * (deepest - self.depth)
        self.lag_end = self.lag_total + 3
        self.ticks = self.total + 1 + 2 * deepest + 2 + 2 * deepest + 3
        self.att_rows = 2 * self.att_src.shape[0]
        self.blocks = self.down_dst.shape[1] // LANES

    def view(self, buf, slot, att):
        return buf.at[slot, pl.ds(0, self.att_rows)] if att else buf.at[slot]

    def each(self, chunk, body):
        slot = lax.rem(jnp.maximum(chunk, 0), SLOTS)
        pl.when((chunk >= 0) & (chunk < self.first))(lambda: body(chunk, slot, False))
        if self.second:
            pl.when((chunk >= self.first) & (chunk < self.total))(lambda: body(chunk, slot, True))

    def send(self, src, dst, sems, target, slot, att):
        return pltpu.make_async_remote_copy(
            src_ref=self.view(src, slot, att),
            dst_ref=self.view(dst, slot, att),
            send_sem=sems[0].at[slot],
            recv_sem=sems[1].at[slot],
            device_id={"ctx": target},
            device_id_type=MESH,
        )

    def to_total(self, slot, att):
        return self.send(self.sums, self.rin, (self.in_send, self.rin_sem), self.inward, slot, att)

    def to_partial(self, slot, att):
        return self.send(
            self.sums, self.rout, (self.in_send, self.rout_sem), self.inward, slot, att
        )

    def to_outward(self, slot, att):
        return self.send(
            self.done, self.rin, (self.out_send, self.rin_sem), self.outward, slot, att
        )

    def load(self, chunk, slot):
        return pltpu.make_async_copy(
            self.mlp_src.at[chunk], self.own.at[slot], self.load_sem.at[slot]
        )

    def stores(self, chunk, slot, att):
        if att:
            rows = self.att_rows // 2
            wide = self.query_dst.shape[1] // LANES
            pairs = []
            for i in range(2):
                at = 2 * (chunk - self.first) + i
                src = self.done.at[slot, pl.ds(i * rows, rows)]
                sem = self.store_sem.at[slot, i]
                q_at = pl.multiple_of(jnp.minimum(at, wide - 1) * LANES, LANES)
                o_at = pl.multiple_of(jnp.maximum(at - wide, 0) * LANES, LANES)
                pairs.append(
                    (
                        at < wide,
                        pltpu.make_async_copy(src, self.query_dst.at[:, pl.ds(q_at, LANES)], sem),
                    )
                )
                pairs.append(
                    (
                        at >= wide,
                        pltpu.make_async_copy(src, self.output_dst.at[:, pl.ds(o_at, LANES)], sem),
                    )
                )
            return pairs
        kind = chunk // self.blocks
        at = pl.multiple_of(lax.rem(chunk, self.blocks) * LANES, LANES)
        sem = self.store_sem.at[slot, 0]
        return [
            (kind == i, pltpu.make_async_copy(self.done.at[slot], dst.at[:, pl.ds(at, LANES)], sem))
            for i, dst in enumerate((self.gate_dst, self.up_dst, self.down_dst))
        ]

    def tick(self, i):
        self.each(i - self.lag_sum + 1, self.stage_load)
        self.each(i - self.lag_sum, self.stage_sum)
        self.each(i - self.lag_sent, self.stage_sent)
        self.each(i - self.lag_total, self.stage_total)
        self.each(i - self.lag_end, self.stage_end)

    def stage_load(self, chunk, slot, att):
        if not att:
            self.load(chunk, slot).start()

    def stage_sum(self, chunk, slot, att):
        if not att:
            self.load(chunk, slot).wait()

        def own():
            if not att:
                return self.own[slot]
            at = (chunk - self.first) * 2 * LANES
            return jnp.concatenate(
                [
                    self.att_src[:, pl.ds(pl.multiple_of(at + i * LANES, LANES), LANES)]
                    for i in range(2)
                ],
                0,
            )

        @pl.when(self.has_out)
        def _():
            self.to_partial(slot, att).wait_recv()
            arrived = self.view(self.rout, slot, att)[...].astype(F32)
            self.view(self.sums, slot, att)[...] = (own().astype(F32) + arrived).astype(BF16)

            @pl.when(chunk < self.total - SLOTS)
            def _():
                pl.semaphore_signal(
                    self.credit_in, 1, device_id={"ctx": self.outward}, device_id_type=MESH
                )

        @pl.when(jnp.logical_not(self.has_out))
        def _():
            self.view(self.sums, slot, att)[...] = own()

        @pl.when(chunk >= SLOTS)
        def _():
            pl.semaphore_wait(self.credit_in, 1)

        pl.when(self.is_mid)(lambda: self.to_total(slot, att).start())
        pl.when(jnp.logical_not(self.is_mid))(lambda: self.to_partial(slot, att).start())

    def stage_sent(self, chunk, slot, att):
        self.to_total(slot, att).wait_send()

    def stage_total(self, chunk, slot, att):
        self.to_total(slot, att).wait_recv()
        arrived = self.view(self.rin, slot, att)
        done = self.view(self.done, slot, att)

        @pl.when(self.is_mid)
        def _():
            mine = self.view(self.sums, slot, att)[...].astype(F32)
            done[...] = (mine + arrived[...].astype(F32)).astype(BF16)

            @pl.when(chunk < self.total - SLOTS)
            def _():
                pl.semaphore_signal(
                    self.credit_in, 1, device_id={"ctx": self.inward}, device_id_type=MESH
                )

        @pl.when(jnp.logical_not(self.is_mid))
        def _():
            done[...] = arrived[...]

            @pl.when(chunk < self.total - SLOTS)
            def _():
                pl.semaphore_signal(
                    self.credit_out, 1, device_id={"ctx": self.inward}, device_id_type=MESH
                )

        @pl.when(self.has_out)
        def _():
            @pl.when(chunk >= SLOTS)
            def _():
                pl.semaphore_wait(self.credit_out, 1)

            self.to_outward(slot, att).start()

        for condition, copy in self.stores(chunk, slot, att):
            pl.when(condition)(copy.start)

    def stage_end(self, chunk, slot, att):
        pl.when(self.has_out)(lambda: self.to_outward(slot, att).wait_send())
        for condition, copy in self.stores(chunk, slot, att):
            pl.when(condition)(copy.wait)


def chip_at(place):
    return 2 * (place // 2) + lax.rem(place + place // 2, 2)


class Ring:
    def __init__(self, count, index):
        self.chips = count // 2
        chip = index // 2
        self.core = lax.rem(index, 2)
        self.place = chip_at(chip)
        self.partner = 2 * chip + 1 - self.core
        self.right = self.device(1)
        self.left = self.device(-1)

    def device(self, offset, core=None):
        place = lax.rem(self.place + offset + self.chips, self.chips)
        return 2 * chip_at(place) + (self.core if core is None else core)


class RingGather:
    def __init__(self, ring, source, slots, sems):
        self.ring, self.source, self.slots = ring, source, slots
        self.sems = sems
        self.far = ring.chips // 2
        self.rows = slots.shape[1]

    def copy(self, offset, target, kind, index, half=None):
        block = self.ring.device(offset)
        src = self.source if offset == 0 else self.slots.at[block]
        dst = self.slots.at[block]
        if half is not None:
            rows = pl.ds(half * (self.rows // 2), self.rows // 2)
            src, dst = src.at[rows], dst.at[rows]
        return pltpu.make_async_remote_copy(
            src_ref=src,
            dst_ref=dst,
            send_sem=self.sems[2 * kind].at[index],
            recv_sem=self.sems[2 * kind + 1].at[index],
            device_id={"fsdp": target},
            device_id_type=MESH,
        )

    def rightward(self, s):
        return self.copy(-s, self.ring.right, 0, s, 0 if s + 1 == self.far else None)

    def leftward(self, s):
        return self.copy(s, self.ring.left, 1, s, 1 if s + 1 == self.far else None)

    def across(self, offset):
        index = 0 if offset == 0 else 2 * abs(offset) - (1 if offset < 0 else 0)
        return self.copy(offset, self.ring.partner, 2, index)

    def arrived(self, s):
        half = self.far == s
        self.copy(-s, self.ring.right, 0, s - 1, 0 if half else None).wait_recv()
        self.copy(s, self.ring.left, 1, s - 1, 1 if half else None).wait_recv()

    def offsets(self, s):
        return [s] if s == self.far else [-s, s]

    def begin(self):
        self.rightward(0).start()
        self.leftward(0).start()
        self.across(0).start()

    def advance(self, s):
        self.arrived(s)
        if s < self.far:
            self.rightward(s).start()
            self.leftward(s).start()
        for offset in self.offsets(s):
            self.across(offset).start()

    def from_partner(self, offset):
        block = self.ring.device(offset, 1 - self.ring.core)
        index = 0 if offset == 0 else 2 * abs(offset) - (1 if offset < 0 else 0)
        pltpu.make_async_remote_copy(
            src_ref=self.slots.at[block],
            dst_ref=self.slots.at[block],
            send_sem=self.sems[4].at[index],
            recv_sem=self.sems[5].at[index],
            device_id={"fsdp": self.ring.partner},
            device_id_type=MESH,
        ).wait_recv()

    def end(self):
        for s in range(self.far):
            self.rightward(s).wait_send()
            self.leftward(s).wait_send()
        self.across(0).wait_send()
        for s in range(1, self.far + 1):
            for offset in self.offsets(s):
                self.across(offset).wait_send()


def gather_sems(chips):
    far = chips // 2
    dma = pltpu.SemaphoreType.DMA
    return [dma((far,))] * 4 + [dma((2 * far + 1,))] * 2


class RingSum:
    def __init__(self, ring, partial, arena, rows, cols, sems):
        self.ring, self.partial = ring, partial
        self.arena, self.rows, self.cols = arena, rows, cols
        (
            self.stage_send,
            self.pair_recv,
            self.right_send,
            self.right_recv,
            self.left_send,
            self.left_recv,
        ) = sems
        far = ring.chips // 2
        self.far = far
        offsets = [far]
        for s in range(far - 1, 0, -1):
            offsets += [s, -s]
        self.offsets = offsets + [0]
        self.at = {offset: i for i, offset in enumerate(self.offsets)}

    def view(self, slot, rows=None):
        return self.arena.at[slot, pl.ds(0, self.rows) if rows is None else rows, pl.ds(0, self.cols)]

    def stage(self, i):
        return self.view(i % 2)

    def pair(self, i, rows=None):
        return self.view(2 + i, rows)

    def side(self, right, s, rows=None):
        return self.view(2 + self.ring.chips + (0 if right else self.far) + s - 1, rows)

    def half(self, which):
        return pl.ds(which * (self.rows // 2), self.rows // 2)

    def pair_copy(self, i):
        return pltpu.make_async_remote_copy(
            src_ref=self.stage(i),
            dst_ref=self.pair(i),
            send_sem=self.stage_send.at[i],
            recv_sem=self.pair_recv.at[i],
            device_id={"fsdp": self.ring.partner},
            device_id_type=MESH,
        )

    def by_columns(self, piece):
        wide = 4 * LANES

        def body(j, _):
            piece(pl.ds(pl.multiple_of(j * wide, wide), wide))
            return 0

        lax.fori_loop(0, self.cols // wide, body, 0)

    def pair_step(self, i):
        offset = self.offsets[i]
        if i >= 2:
            self.pair_copy(i - 2).wait_send()
        owner = self.ring.device(offset, 1 - self.ring.core)
        rows = pl.ds(0, self.rows)

        def piece(at):
            self.arena[i % 2, rows, at] = self.partial(owner, at).astype(BF16)

        self.by_columns(piece)
        self.pair_copy(i).start()

    def pair_add(self, i):
        owner = self.ring.device(self.offsets[i])
        self.pair_copy(i).wait_recv()
        rows = pl.ds(0, self.rows)

        def piece(at):
            mine = self.partial(owner, at)
            there = (2 + i, rows, at)
            self.arena[there] = (mine + self.arena[there].astype(F32)).astype(BF16)

        self.by_columns(piece)

    def pair_all(self, between=None):
        last = len(self.offsets)
        for i in range(last):
            self.pair_step(i)
            if i >= 1:
                self.pair_add(i - 1)
                self.launch_free(i - 1)
            if between is not None:
                between(i)
        self.pair_add(last - 1)
        for i in range(max(last - 2, 0), last):
            self.pair_copy(i).wait_send()

    def hop(self, s, right, which):
        owner = self.at[s if right or s == self.far else -s]
        rows = self.half(which)
        return pltpu.make_async_remote_copy(
            src_ref=self.pair(owner, rows),
            dst_ref=self.side(right, s, rows),
            send_sem=(self.right_send if right else self.left_send).at[s - 1, which],
            recv_sem=(self.right_recv if right else self.left_recv).at[s - 1, which],
            device_id={"fsdp": self.ring.right if right else self.ring.left},
            device_id_type=MESH,
        )

    def hops(self):
        far = self.far
        moves = [(far, True, 0), (far, False, 1)]
        if far > 1:
            moves += [(far - 1, True, 1), (far - 1, False, 0)]
            moves += [(far - 1, True, 0), (far - 1, False, 1)]
        for s in range(far - 2, 0, -1):
            for which in range(2):
                moves += [(s, True, which), (s, False, which)]
        return moves

    def free(self, s, right, which):
        return s == self.far or (s == self.far - 1 and which == (1 if right else 0))

    def launch_free(self, i):
        offset = self.offsets[i]
        for s, right, which in self.hops():
            owner = s if right or s == self.far else -s
            if self.free(s, right, which) and owner == offset:
                self.hop(s, right, which).start()

    def launch(self):
        for s, right, which in self.hops():
            if not self.free(s, right, which):
                self.hop(s + 1, right, which).wait_recv()
                owner = self.at[s if right else -s]
                rows = self.half(which)
                arrived = self.side(right, s + 1, rows)
                mine = self.pair(owner, rows)
                mine[...] = (mine[...].astype(F32) + arrived[...].astype(F32)).astype(BF16)
                self.hop(s, right, which).start()

    def finish(self):
        for s, right, which in self.hops():
            if s == 1:
                self.hop(s, right, which).wait_recv()
            self.hop(s, right, which).wait_send()

    def by_rows(self, piece):
        step = self.rows // 4

        def body(i, _):
            piece(pl.ds(pl.multiple_of(i * step, step), step))
            return 0

        lax.fori_loop(0, 4, body, 0)

    def value(self, rows):
        own = self.pair(self.at[0], rows)[...].astype(F32)
        left = self.side(True, 1, rows)[...].astype(F32)
        return own + left + self.side(False, 1, rows)[...].astype(F32)


def sum_sems(chips):
    far = chips // 2
    dma = pltpu.SemaphoreType.DMA
    return [dma((chips,))] * 2 + [dma((far, 2))] * 4


def back_kernel(
    sizes,
    a2_ref,
    cot_ref,
    wgate_ref,
    wup_ref,
    wdown_ref,
    wout_ref,
    wqkv_ref,
    h1_ref,
    q_in,
    o_in,
    a1_in,
    x_in,
    k_in,
    v_in,
    lse_in,
    mask_in,
    turn_in,
    gain1_ref,
    gain2_ref,
    result_out,
    gtok_out,
    gains_ref,
    gate_out,
    up_out,
    down_out,
    query_out,
    output_out,
    rows_all,
    gz_ref,
    *scratch,
):
    ctx_n, fsdp_n = sizes
    (
        zown,
        zrout,
        zsums,
        zrin,
        zdone,
        az,
        arena,
        dh1,
        gqkv,
        dkv,
        dkv_in,
        gslot,
        cslot,
    ) = scratch[:13]
    scratch = scratch[13:]
    zsems, scratch = scratch[:8], scratch[8:]
    gsems, scratch = scratch[:6], scratch[6:]
    da2_sems, scratch = scratch[:6], scratch[6:]
    out_sems, scratch = scratch[:6], scratch[6:]
    ysems, scratch = scratch[:6], scratch[6:]
    xsems, scratch = scratch[:6], scratch[6:]
    (
        dkv_send,
        dkv_recv,
        gain_send,
        gain_recv,
        cgain_send,
        cgain_recv,
        wsem,
        isem,
        ssem,
        ready,
    ) = scratch
    ctx = lax.axis_index("ctx")
    fsdp = lax.axis_index("fsdp")
    ring = Ring(fsdp_n, fsdp)
    count, width = a2_ref.shape
    block = count // 2
    keys = k_in.shape[0] // 2
    scale = HD ** (-0.5)
    shard = query_out.shape[0]
    cols = gqkv.shape[1]
    local = wgate_ref.shape[0]
    key_cols = KV * HD

    barrier = pltpu.get_barrier_semaphore()
    for axis, me, n in (("ctx", ctx, ctx_n), ("fsdp", fsdp, fsdp_n)):
        for step in range(1, n):
            pl.semaphore_signal(
                barrier, 1, device_id={axis: lax.rem(me + step, n)}, device_id_type=MESH
            )
    pl.semaphore_wait(barrier, ctx_n + fsdp_n - 2)

    rounds = [0]

    def settle():
        sem = ready.at[rounds[0]]
        rounds[0] += 1
        for target in (ring.partner, ring.left, ring.right):
            pl.semaphore_signal(sem, 1, device_id={"fsdp": target}, device_id_type=MESH)
        pl.semaphore_wait(sem, 3)

    line = LineSum(
        ctx_n,
        ctx,
        gz_ref.shape[0],
        az.shape[1] // (2 * LANES),
        (gz_ref, az),
        (gate_out, up_out, down_out, query_out, output_out),
        (zown, zrout, zsums, zrin, zdone),
        zsems,
    )
    clock = [0]

    def ticks(number):
        start = clock[0]
        clock[0] = start + number

        def body(i, _):
            line.tick(i)
            return 0

        lax.fori_loop(start, start + number, body, 0)

    gather = RingGather(ring, a2_ref, rows_all, gsems)
    gather.begin()

    def ring_sum(partial, rows, wide, sems):
        return RingSum(ring, partial, arena, rows, wide, sems)

    def feed_forward(wgate, wup, wdown, hb, abuf, cbuf, stage):
        loads = [
            pltpu.make_async_copy(wdown_ref, wdown, isem.at[0]),
            pltpu.make_async_copy(wgate_ref, wgate, isem.at[1]),
            pltpu.make_async_copy(wup_ref, wup, isem.at[2]),
            pltpu.make_async_copy(a2_ref, rows_all.at[fsdp], isem.at[3]),
            pltpu.make_async_copy(a2_ref, abuf.at[0], isem.at[4]),
            pltpu.make_async_copy(h1_ref, dh1, isem.at[5]),
        ]

        def cot_load(f):
            slot = 2 + lax.rem(f, 2)
            return pltpu.make_async_copy(cot_ref.at[f], abuf.at[slot], wsem.at[slot - 2])

        cot_load(0).start()
        for load in loads:
            load.start()
        loads[0].wait()

        def dhid(f, _):
            pl.when(f + 1 < fsdp_n)(lambda: cot_load(f + 1).start())
            cot_load(f).wait()
            hb[2, f] = through(abuf[2 + lax.rem(f, 2)], wdown[...]).astype(BF16)
            return 0

        lax.fori_loop(0, fsdp_n, dhid, 0)
        for load in loads[1:]:
            load.wait()

        def fetch(f, slot):
            return pltpu.make_async_copy(rows_all.at[f], abuf.at[slot], isem.at[slot])

        def gates(f, slot):
            rows = abuf[slot]
            hidden, dgate, dup = gate_back(
                hb[2, f].astype(F32), through(rows, wgate[...]), through(rows, wup[...])
            )
            hb[0, f] = dgate
            hb[1, f] = dup
            hb[2, f] = hidden

        gates(fsdp, 0)
        gather.from_partner(0)
        fetch(ring.partner, 1).start()
        fetch(ring.partner, 1).wait()
        gates(ring.partner, 1)
        for s in range(1, gather.far + 1):
            gather.advance(s)
            offsets = gather.offsets(s)
            blocks = [ring.device(offset) for offset in offsets]
            blocks += [ring.device(offset, 1 - ring.core) for offset in offsets]
            for i in range(len(offsets)):
                fetch(blocks[i], i).start()
            for i, offset in enumerate(offsets):
                gather.from_partner(offset)
                fetch(blocks[len(offsets) + i], len(offsets) + i).start()

            def each(i, _, blocks=blocks):
                f = blocks[0]
                for j in range(1, len(blocks)):
                    f = jnp.where(i == j, blocks[j], f)
                fetch(f, i).wait()
                gates(f, i)
                return 0

            lax.fori_loop(0, len(blocks), each, 0)
        gather.end()

        wide = 2 * LANES
        per_kind = width // wide
        total = 3 * per_kind

        def chunk_load(m, start):
            slot = lax.rem(m, 2)
            at = pl.multiple_of(lax.rem(m, per_kind) * wide, wide)
            for source, use in ((rows_all, m < 2 * per_kind), (cot_ref, m >= 2 * per_kind)):
                copy = pltpu.make_async_copy(
                    source.at[:, :, pl.ds(at, wide)], cbuf.at[slot], wsem.at[slot]
                )
                pl.when(use)(copy.start if start else copy.wait)

        def chunk_store(m):
            slot = lax.rem(m, 2)
            return pltpu.make_async_copy(
                stage.at[slot], gz_ref.at[pl.ds(2 * m, 2)], ssem.at[slot]
            )

        def gradients(m, lo):
            slot = lax.rem(m, 2)
            pl.when(m + 1 < total)(lambda: chunk_load(jnp.minimum(m + 1, total - 1), True))
            chunk_load(m, False)
            right = cbuf[slot].reshape(fsdp_n * count, wide)
            left = hb[m // per_kind].reshape(fsdp_n * count, local)
            out = across(left, right).astype(BF16)
            pl.when(m >= lo + 2)(lambda: chunk_store(jnp.maximum(m - 2, 0)).wait())
            stage[slot, 0] = out[:, :LANES]
            stage[slot, 1] = out[:, LANES:]
            chunk_store(m).start()

        def run(lo, hi, every=0):
            start = clock[0]

            def body(m, _):
                gradients(m, lo)
                if every:
                    pl.when(lax.rem(m - lo, every) == every - 1)(
                        lambda: line.tick(start + (m - lo) // every)
                    )
                return 0

            lax.fori_loop(lo, hi, body, 0)
            for m in (hi - 2, hi - 1):
                chunk_store(jnp.int32(m)).wait()
            if every:
                clock[0] = start + (hi - lo) // every

        chunk_load(jnp.int32(0), True)
        head = 4
        run(0, head)
        ticks(3)

        def da2_partial(f, at):
            return matmul(hb[0, f], wgate[:, at]) + matmul(hb[1, f], wup[:, at])

        da2 = ring_sum(da2_partial, count, width, da2_sems)
        da2.pair_all(lambda i: ticks(1) if i < 3 else None)
        middle = head + (total - head) // 2
        run(head, middle, 3)
        da2.launch()
        run(middle, total, 3)
        own_cot = pltpu.make_async_copy(cot_ref.at[fsdp], abuf.at[0], isem.at[0])
        own_cot.start()
        da2.finish()
        own_cot.wait()
        gain = gain2_ref[...]
        piece = count // 4

        def norm_back(i, acc):
            rows = pl.ds(pl.multiple_of(i * piece, piece), piece)
            hidden = dh1[rows]
            grad = da2.value(rows)
            factor = lax.rsqrt(jnp.mean(hidden * hidden, -1, keepdims=True) + EPSILON)
            unit = hidden * factor
            dh1[rows] = abuf[0, rows].astype(F32) + normed_back(unit, factor, grad, gain)
            return acc + jnp.sum(grad * unit, 0, keepdims=True)

        gain2_sum = lax.fori_loop(0, 4, norm_back, jnp.zeros((1, width), F32))
        gslot[fsdp, 1:2] = gain2_sum
        settle()

        def out_partial(f, at):
            return matmul(hb[2, f], wdown[:, at])

        mlp_out = ring_sum(out_partial, count, width, out_sems)
        mlp_out.pair_all(lambda i: ticks(1))
        holder.append(mlp_out)

    holder = []
    pl.run_scoped(
        feed_forward,
        pltpu.VMEM((local, width), BF16),
        pltpu.VMEM((local, width), BF16),
        pltpu.VMEM((local, width), BF16),
        pltpu.VMEM((3, fsdp_n, count, local), BF16),
        pltpu.VMEM((4, count, width), BF16),
        pltpu.VMEM((2, fsdp_n, count, 2 * LANES), BF16),
        pltpu.VMEM((2, 2, local, LANES), BF16),
    )
    mlp_out = holder[0]

    def attention_back(
        q_ref, o_ref, do_ref, a1_ref, dhb_ref, k_ref, v_ref, lse_ref, mask_ref, turn_ref,
        h1_buf, obuf, wbuf, kz, vz, dk_acc, dv_acc,
    ):
        loads = [
            pltpu.make_async_copy(src, dst, isem.at[i])
            for i, (src, dst) in enumerate(
                [
                    (q_in, q_ref),
                    (o_in, o_ref),
                    (a1_in, a1_ref),
                    (k_in, k_ref),
                    (v_in, v_ref),
                    (lse_in, lse_ref),
                    (mask_in, mask_ref),
                    (turn_in, turn_ref),
                ]
            )
        ]

        def wout_load(f):
            return pltpu.make_async_copy(wout_ref.at[f], obuf.at[f % 2], wsem.at[f % 2])

        wout_load(0).start()
        for load in loads:
            load.start()
        dhb_ref[...] = dh1[...].astype(BF16)
        for f in range(fsdp_n):
            if f + 1 < fsdp_n:
                wout_load(f + 1).start()
            wout_load(f).wait()
            term = through(dhb_ref[:, f * shard : (f + 1) * shard], obuf[f % 2])
            h1_buf[...] = term if f == 0 else h1_buf[...] + term
        do_ref[...] = h1_buf[...].astype(BF16)
        h1_load = pltpu.make_async_copy(h1_ref, h1_buf, ssem.at[0])
        h1_load.start()
        ticks(1)
        mlp_out.launch()
        for load in loads:
            load.wait()

        step_keys = min(keys, 4 * LANES)

        def piece(par, q4, do4, lse, delta, at, mask, grad_q):
            span = pl.ds(at, step_keys)
            k_part = kz[par, span]
            v_part = vz[par, span]
            scores = through(q4, k_part)
            if mask is not None:
                scores = scores + mask
            probs = jnp.exp(scores - lse)
            dprob = through(do4, v_part)
            dscore = (probs * (dprob - delta)).astype(BF16)
            dk_acc[par, span] += across(dscore, q4)
            dv_acc[par, span] += across(probs.astype(BF16), do4)
            return grad_q + matmul(dscore, k_part)

        def group_step(group, rb):
            rows = pl.ds(rb * block, block)
            q4 = stacked(q_ref, rows, group) * jnp.asarray(scale, BF16)
            do4 = stacked(do_ref, rows, group)
            prod = do4.astype(F32) * stacked(o_ref, rows, group).astype(F32)
            lse_all = lse_ref[rb]
            grad_q = jnp.zeros((PAIRS * block, LANES), F32)
            for par in range(2):
                lse = jnp.sum(
                    jnp.where(lanes_of(lse_all.shape) == 2 * group + par, lse_all, 0.0),
                    -1,
                    keepdims=True,
                )
                delta = jnp.sum(
                    jnp.where(lanes_of(prod.shape) // HD == par, prod, 0.0), -1, keepdims=True
                )
                for at in range(0, (rb + 1) * keys, step_keys):
                    mask = None
                    if at >= rb * keys:
                        mask = mask_ref[rb, :, pl.ds(at - rb * keys, step_keys)]
                        mask = jnp.concatenate([mask] * PAIRS, 0)
                    grad_q = piece(par, q4, do4, lse, delta, at, mask, grad_q)
            grad_q = grad_q * scale
            cosine, sine = turn_ref[0, rows], turn_ref[1, rows]
            for j in range(PAIRS):
                part = grad_q[j * block : (j + 1) * block]
                at = pl.multiple_of((group * PAIRS + j) * LANES, LANES)
                gqkv[rows, pl.ds(at, LANES)] = (part * cosine - turned(part) * sine).astype(BF16)

        def dkv_copy(owner, tile, step):
            return pltpu.make_async_remote_copy(
                src_ref=dkv.at[owner, tile],
                dst_ref=dkv_in.at[ctx, tile],
                send_sem=dkv_send.at[step, tile],
                recv_sem=dkv_recv.at[step, tile],
                device_id={"ctx": owner},
                device_id_type=MESH,
            )

        def attention(lo, hi):
            start = clock[0]

            def body(group, _):
                spread_heads(k_ref, kz, group)
                spread_heads(v_ref, vz, group)
                dk_acc[...] = jnp.zeros_like(dk_acc)
                dv_acc[...] = jnp.zeros_like(dv_acc)
                for rb in range(2):
                    group_step(group, rb)
                    line.tick(start + (group - lo) * 2 + rb)
                tile = group // 2
                for which, acc in enumerate((dk_acc, dv_acc)):
                    for part in range(ctx_n):
                        for rb in range(2):
                            span = pl.ds(rb * keys + part * block, block)
                            both = jnp.where(
                                lanes_of((block, LANES)) < HD, acc[0, span], acc[1, span]
                            )
                            both = both + roll_lanes(both, HD)
                            there = (part, tile, which, pl.ds(rb * block, block))
                            mine = lanes_of((block, LANES)) // HD == lax.rem(group, 2)
                            dkv[there] = jnp.where(mine, both.astype(BF16), dkv[there])
                return 0

            lax.fori_loop(lo, hi, body, 0)
            clock[0] = start + (hi - lo) * 2

        def send_dkv(tile):
            for step in range(1, ctx_n):
                dkv_copy(lax.rem(ctx + step, ctx_n), tile, step - 1).start()

        attention(0, 2)
        send_dkv(0)
        mlp_out.finish()
        h1_load.wait()

        def add_out(rows):
            h1_buf[rows] = h1_buf[rows] + mlp_out.value(rows)

        mlp_out.by_rows(add_out)
        settle()

        def output_partial(f, at):
            return across(dhb_ref[:, pl.ds(pl.multiple_of(f * shard, shard), shard)], o_ref[:, at])

        ysum = ring_sum(output_partial, shard, width, ysems)
        ysum.pair_all(lambda i: ticks(1))
        attention(2, 3)
        ysum.launch()
        attention(3, 4)
        send_dkv(1)
        ticks(2)
        do_ref[...] = h1_buf[...].astype(BF16)
        result_copy = pltpu.make_async_copy(do_ref, result_out, isem.at[0])
        result_copy.start()
        ysum.finish()

        def keep_output(rows):
            az[rows, cols:] = ysum.value(rows).astype(BF16)

        ysum.by_rows(keep_output)
        settle()
        x_load = pltpu.make_async_copy(x_in, q_ref, isem.at[1])
        x_load.start()

        for step in range(1, ctx_n):
            for tile in range(KV // 2):
                dkv_copy(lax.rem(ctx + step, ctx_n), tile, step - 1).wait_send()
                sender = lax.rem(ctx - step + ctx_n, ctx_n)
                pltpu.make_async_remote_copy(
                    src_ref=dkv.at[sender, tile],
                    dst_ref=dkv_in.at[sender, tile],
                    send_sem=dkv_send.at[step - 1, tile],
                    recv_sem=dkv_recv.at[step - 1, tile],
                    device_id={"ctx": sender},
                    device_id_type=MESH,
                ).wait_recv()
        cosine, sine = turn_ref[0], turn_ref[1]
        for tile in range(KV // 2):
            for which in range(2):
                part = dkv[ctx, tile, which].astype(F32)
                for step in range(1, ctx_n):
                    part = part + dkv_in[lax.rem(ctx + step, ctx_n), tile, which].astype(F32)
                if which == 0:
                    part = part * cosine - turned(part) * sine
                at = width + which * key_cols + tile * LANES
                gqkv[:, at : at + LANES] = part.astype(BF16)

        def query_partial(f, at):
            return across(a1_ref[:, pl.ds(pl.multiple_of(f * shard, shard), shard)], gqkv[:, at])

        xsum = ring_sum(query_partial, shard, cols, xsems)
        xsum.pair_all(lambda i: ticks(1))
        ticks(2)
        xsum.launch()
        ticks(2)

        def weight_copy(f):
            return pltpu.make_async_copy(wqkv_ref.at[f], wbuf.at[f % 2], wsem.at[f % 2])

        weight_copy(0).start()
        for f in range(fsdp_n):
            if f + 1 < fsdp_n:
                weight_copy(f + 1).start()
            weight_copy(f).wait()
            h1_buf[:, f * shard : (f + 1) * shard] = through(gqkv[...], wbuf[f % 2])
        x_load.wait()
        gain = gain1_ref[...]
        piece_rows = count // 4

        def norm_back(i, acc):
            rows = pl.ds(pl.multiple_of(i * piece_rows, piece_rows), piece_rows)
            x = q_ref[rows].astype(F32)
            grad = h1_buf[rows]
            factor = lax.rsqrt(jnp.mean(x * x, -1, keepdims=True) + EPSILON)
            unit = x * factor
            o_ref[rows] = (dh1[rows] + normed_back(unit, factor, grad, gain)).astype(BF16)
            return acc + jnp.sum(grad * unit, 0, keepdims=True)

        gslot[fsdp, 0:1] = lax.fori_loop(0, 4, norm_back, jnp.zeros((1, width), F32))
        gtok_copy = pltpu.make_async_copy(o_ref, gtok_out, isem.at[2])
        gtok_copy.start()

        def gain_copy(slots, axis, here, step, sems):
            n = fsdp_n if axis == "fsdp" else ctx_n
            return pltpu.make_async_remote_copy(
                src_ref=slots.at[here],
                dst_ref=slots.at[here],
                send_sem=sems[0].at[step - 1],
                recv_sem=sems[1].at[step - 1],
                device_id={axis: lax.rem((fsdp if axis == "fsdp" else ctx) + step, n)},
                device_id_type=MESH,
            )

        def exchange(slots, axis, n, me, sems):
            for step in range(1, n):
                gain_copy(slots, axis, me, step, sems).start()
            for step in range(1, n):
                gain_copy(slots, axis, me, step, sems).wait_send()
                gain_copy(slots, axis, lax.rem(me - step + n, n), step, sems).wait_recv()
            total = slots[0]
            for i in range(1, n):
                total = total + slots[i]
            return total

        cslot[ctx] = exchange(gslot, "fsdp", fsdp_n, fsdp, (gain_send, gain_recv))
        gains_ref[...] = exchange(cslot, "ctx", ctx_n, ctx, (cgain_send, cgain_recv))

        xsum.finish()

        def keep_query(rows):
            az[rows, :cols] = xsum.value(rows).astype(BF16)

        xsum.by_rows(keep_query)
        result_copy.wait()
        gtok_copy.wait()

    total_keys = k_in.shape[0]
    rows_type = pltpu.VMEM((count, width), BF16)
    pl.run_scoped(
        attention_back,
        rows_type,
        rows_type,
        rows_type,
        rows_type,
        rows_type,
        pltpu.VMEM(k_in.shape, BF16),
        pltpu.VMEM(v_in.shape, BF16),
        pltpu.VMEM(lse_in.shape, F32),
        pltpu.VMEM(mask_in.shape, F32),
        pltpu.VMEM(turn_in.shape, F32),
        pltpu.VMEM((count, width), F32),
        pltpu.VMEM((2,) + wout_ref.shape[1:], BF16),
        pltpu.VMEM((2,) + wqkv_ref.shape[1:], BF16),
        pltpu.VMEM((2, total_keys, LANES), BF16),
        pltpu.VMEM((2, total_keys, LANES), BF16),
        pltpu.VMEM((2, total_keys, LANES), F32),
        pltpu.VMEM((2, total_keys, LANES), F32),
    )
    ticks(line.ticks - clock[0])


def back(
    a2, cot, w_gate, w_up, w_down, w_out, wqkv, h1, q, o, a1, x, k_all, v_all, lse, mask, turn,
    gain_one, gain_two,
):
    ctx_n = lax.axis_size("ctx")
    fsdp_n = lax.axis_size("fsdp")
    count, width = q.shape
    local = w_gate.shape[0]
    shard, cols = wqkv.shape[1:]
    chips = fsdp_n // 2
    far = chips // 2
    vmem = pl.BlockSpec(memory_space=pltpu.VMEM)
    hbm = pl.BlockSpec(memory_space=pl.ANY)
    dma = pltpu.SemaphoreType.DMA
    regular = pltpu.SemaphoreType.REGULAR
    zbuf = pltpu.VMEM((SLOTS, local, LANES), BF16)
    scratch = (
        [zbuf] * 5
        + [
            pltpu.VMEM((shard, cols + width), BF16),
            pltpu.VMEM((2 + chips + 2 * far, max(count, shard), cols), BF16),
            pltpu.VMEM((count, width), F32),
            pltpu.VMEM((count, cols), BF16),
            pltpu.VMEM((ctx_n, KV // 2, 2, count, LANES), BF16),
            pltpu.VMEM((ctx_n, KV // 2, 2, count, LANES), BF16),
            pltpu.VMEM((fsdp_n, 2, width), F32),
            pltpu.VMEM((ctx_n, 2, width), F32),
        ]
        + [dma((SLOTS,))] * 5
        + [dma((SLOTS, 2)), regular, regular]
        + gather_sems(chips)
        + sum_sems(chips) * 4
        + [
            dma((ctx_n - 1, KV // 2)),
            dma((ctx_n - 1, KV // 2)),
            dma((fsdp_n - 1,)),
            dma((fsdp_n - 1,)),
            dma((ctx_n - 1,)),
            dma((ctx_n - 1,)),
            dma((2,)),
            dma((9,)),
            dma((2,)),
            regular((4,)),
        ]
    )
    return pl.pallas_call(
        functools.partial(back_kernel, (ctx_n, fsdp_n)),
        out_shape=(
            jax.ShapeDtypeStruct((count, width), BF16),
            jax.ShapeDtypeStruct((count, width), BF16),
            jax.ShapeDtypeStruct((2, width), F32),
            jax.ShapeDtypeStruct((local, width), BF16),
            jax.ShapeDtypeStruct((local, width), BF16),
            jax.ShapeDtypeStruct((local, width), BF16),
            jax.ShapeDtypeStruct((shard, cols), BF16),
            jax.ShapeDtypeStruct((shard, width), BF16),
            jax.ShapeDtypeStruct((fsdp_n, count, width), BF16),
            jax.ShapeDtypeStruct((3 * width // LANES, local, LANES), BF16),
        ),
        in_specs=[hbm] * 17 + [vmem] * 2,
        out_specs=(hbm, hbm, vmem) + (hbm,) * 7,
        scratch_shapes=scratch,
        compiler_params=pltpu.CompilerParams(
            collective_id=1, has_side_effects=True, vmem_limit_bytes=VMEM_LIMIT
        ),
        name="back",
    )(
        a2, cot, w_gate, w_up, w_down, w_out, wqkv, h1, q, o, a1, x, k_all, v_all, lse, mask, turn,
        gain_one, gain_two,
    )[:8]


def shards(
    tokens,
    cotangent,
    block_table,
    gain_attn,
    w_query,
    w_key,
    w_value,
    w_output,
    gain_mlp,
    w_gate,
    w_up,
    w_down,
):
    ctx_n = lax.axis_size("ctx")
    ctx = lax.axis_index("ctx")
    count, width = tokens.shape[1:]
    block = count // 2
    local = w_gate.shape[1]

    table = block_table.reshape(ctx_n, 2)
    lower, upper = jnp.min(table, 1), jnp.max(table, 1)
    owned = table[ctx]
    swap = owned[0] > owned[1]

    def ordered(rows):
        return jnp.where(swap, jnp.concatenate([rows[block:], rows[:block]], 0), rows)

    offsets = jnp.arange(block, dtype=jnp.int32)
    spots = jnp.stack([lower, upper])[:, :, None] * block + offsets
    own_spots = spots[:, ctx]
    key_spots = spots.reshape(2, -1)
    mask = jnp.where(own_spots[:, :, None] >= key_spots[:, None, :], 0.0, NEGATIVE).astype(F32)
    freqs = 10000.0 ** (-jnp.arange(HD // 2, dtype=F32) / (HD // 2))
    angle = own_spots.reshape(-1).astype(F32)[:, None] * freqs[None, :]
    angle = jnp.concatenate([angle] * (LANES * 2 // HD), -1)
    turn = jnp.stack([jnp.cos(angle), jnp.sin(angle)])

    rows_in = ordered(tokens[0])
    grad_out = ordered(cotangent[0])

    wqkv = lax.all_gather(jnp.concatenate([w_query, w_key, w_value], 1), "fsdp", axis=0)
    full_output = lax.all_gather(w_output, "fsdp", axis=0)
    inputs = rows_in.astype(F32)
    normal_one = normed(inputs, gain_attn)[2]
    qkv = matmul(normal_one, wqkv.reshape(width, -1))

    def rotary(values):
        heads = values.reshape(count, -1, HD)
        middle = HD // 2
        spun = jnp.concatenate([-heads[..., middle:], heads[..., :middle]], -1)
        cosine, sine = turn[:, :, None, :HD]
        return (heads * cosine + spun * sine).reshape(count, -1).astype(BF16)

    key_cols = KV * HD
    queries = rotary(qkv[:, :width])
    keys_own = rotary(qkv[:, width : width + key_cols])
    values_own = qkv[:, width + key_cols :].astype(BF16)

    def gathered(rows):
        every = lax.all_gather(rows, "ctx", axis=0).reshape(ctx_n, 2, block, key_cols)
        return every.transpose(1, 0, 2, 3).reshape(-1, key_cols)

    keys_all, values_all = gathered(keys_own), gathered(values_own)
    mixed, lse = attend(queries, keys_all, values_all, mask)
    attn_out = lax.dot_general(
        mixed, full_output, (((1,), (1,)), ((), ())), preferred_element_type=F32
    ).reshape(count, width)
    hidden_one = inputs + attn_out
    normal_two = normed(hidden_one, gain_mlp)[2]
    grad_all = lax.all_gather(grad_out, "fsdp", axis=0)
    result, grad_tokens, gains, gate_sum, up_sum, down_sum, query_sum, output_sum = back(
        normal_two,
        grad_all,
        w_gate.T,
        w_up.T,
        w_down,
        full_output,
        wqkv,
        hidden_one,
        queries,
        mixed,
        normal_one,
        rows_in,
        keys_all,
        values_all,
        lse,
        mask,
        turn,
        gain_attn[None],
        gain_mlp[None],
    )
    query_sum = query_sum.astype(F32)
    return (
        ordered(result)[None],
        ordered(grad_tokens)[None],
        query_sum[:, :width],
        query_sum[:, width : width + key_cols],
        query_sum[:, width + key_cols :],
        output_sum.T.astype(F32),
        gate_sum.astype(F32).T,
        up_sum.astype(F32).T,
        down_sum.astype(F32),
        gains[0],
        gains[1],
    )


def solution(mesh):
    in_specs = (
        P("fsdp", "ctx", None),
        P("fsdp", "ctx", None),
        P(),
        P(),
        P("fsdp", None),
        P("fsdp", None),
        P("fsdp", None),
        P(None, "fsdp"),
        P(),
        P(None, "fsdp"),
        P(None, "fsdp"),
        P("fsdp", None),
    )
    out_specs = (
        P("fsdp", "ctx", None),
        P("fsdp", "ctx", None),
        P("fsdp", None),
        P("fsdp", None),
        P("fsdp", None),
        P(None, "fsdp"),
        P(None, "fsdp"),
        P(None, "fsdp"),
        P("fsdp", None),
        P(),
        P(),
    )
    return jax.shard_map(shards, mesh=mesh, in_specs=in_specs, out_specs=out_specs, check_vma=False)
```

time: 811 us -> 612 us (0.75)
  waiting for transfers between devices: 203 us -> 76.3 us
  matrix products: 119 us -> 14.6 us
  Pallas kernels: 331 us -> 402 us
  local copies, waits for them, and re-layouts: 60 us -> 32.2 us
  other arithmetic: 43.4 us -> 32.3 us
    dot_general x10 -> x1, matrix products: 104 us -> 6.1 us  [dot(): lax.dot_general(left, right, (((left_dim,), (right_dim,)), ((), ())), pre...]
    reduce_scatter x2 -> x0, waiting for transfers between devices: 95.5 us -> none  [scattered(): lax.psum_scatter(partial.astype(BF16), 'fsdp', scatter_dimension=0, tiled...]
    pallas_call x1, Pallas kernels: 316 us -> 387 us  [back(): pl.pallas_call(functools.partial(back_kernel, (ctx_n, fsdp_n)), out_shape...]
    all_gather x2 -> x1, waiting for transfers between devices: 67 us -> 23.5 us  [shards(): grad_all = lax.all_gather(grad_out, 'fsdp', axis=0)]
    all_gather x1, waiting for transfers between devices: 40 us -> 52.1 us  [shards(): lax.all_gather(jnp.concatenate([w_query, w_key, w_value], 1), 'fsdp', axi...]
    unnamed x75 -> x43, local copies, waits for them, and re-layouts: 19.8 us -> 8.31 us
  transfers between devices with their start and end apart: 6 -> 3, of which waited for: 5 -> 2; matrix products, arithmetic and copies ran while one was open for 16% -> 9% of each run, Pallas kernels for 2% -> 3%
where the time goes in v3:
time: 612 us; the launch traced here: 606 us
  Pallas kernels  402 us (66%)
  waiting for transfers between devices  76.3 us (12%)
  blocking collectives  32.5 us (5%)
  other arithmetic  32.3 us (5%)
  local copies, waits for them, and re-layouts  32.2 us (5%)
  between operations  15.6 us (3%)
  matrix products  14.6 us (2%)
    pallas_call x1, Pallas kernels, back(): pl.pallas_call(functools.partial(back_kernel, (ctx_n, fsdp_n)), out_shape...  387 us
    all_gather x1, waiting for transfers between devices, shards(): lax.all_gather(jnp.concatenate([w_query, w_key, w_value], 1), 'fsdp', axi...  52.1 us
    all_gather x2, blocking collectives, gathered(): lax.all_gather(rows, 'ctx', axis=0).reshape(ctx_n, 2, block, key_cols)  32.5 us
    all_gather x1, waiting for transfers between devices, shards(): grad_all = lax.all_gather(grad_out, 'fsdp', axis=0)  23.5 us
    pallas_call x1, Pallas kernels, attend(): pl.pallas_call(attend_kernel, out_shape=(jax.ShapeDtypeStruct((count, H *...  15.3 us
  transfers between devices with their start and end apart: 3, of which 2 were waited for; matrix products, arithmetic and copies ran while one was open for 9% of the time, Pallas kernels for 3%

profile of v3, /device:TPU:0, one launch (start us, length us, event | category | flops | bytes accessed | tf_op | source)
XLA Modules:
  0.0 605.6 jit_solution(1588778854812662913)
XLA Ops:
  7.2 2.6 pad_maximum_fusion
  9.9 0.7 all-gather.12.cloned.1.call-update
  10.8 0.6 fusion.25
  12.8 1.4 maximum_select_fusion.4
  14.2 0.1 fusion.19
  14.6 0.6 fusion.16
  15.4 0.8 copy.55
  16.2 1.3 copy.65
  17.5 0.2 mul.157
  17.8 1.8 copy.50
  19.6 0.3 slice_bitcast_fusion.3
  19.9 1.1 copy.70
  21.0 1.0 copy.69
  22.0 0.7 pad_maximum_fusion.1.turn_in
  22.7 0.5 fusion
  23.3 1.1 compare_select_fusion.mask_ref.mask_in
  24.4 52.1 %all-gather.10.cloned.1.call-done = bf16[2048,2560]{1,0:T(8,128)(2,1)} async-done(((bf16[256,2560]{1,0:T(8,128)(2,1)}), bf16[2048,2560]{1,0:T(8,128)(2,1)}) %all-gather.10.cloned.1.call-update) | async-done | bytes 10485776 | tf_op jit(solution)/shard_map/all_gather | solution.py:1310
  76.5 6.1 %fusion.4 = f32[256,2560]{1,0:T(8,128)S(1)} fusion(bf16[2048,2560]{1,0:T(8,128)(2,1)} %all-gather.10.cloned.1.call-done, bf16[1,256,2048]{2,1,0:T(8,128)(2,1)S(1)} %copy-done, bf16[1,128,2048]{2,1,0:T(8,128)(2,1)} %copy-done.9, bf16[1,128,2048]{2,1,0:T(8,128)(2,1)} %copy-done.10, f32[2048]{0:T(1024)S(1)} %copy-done.17, f32[256]{0:T(256)S(1)} %add_rsqrt_fusion.1, ...), kind=kOutput, calls=%fused_computation.16 | convolution fusion | flops 2689073152 | bytes 15213569 | tf_op jit(solution)/shard_map/dot_general | solution.py:27
  82.7 1.4 copy-done.2
  84.1 1.5 slice.109
  85.9 0.7 copy-done.12
  86.6 1.0 add_convert_fusion.1
  87.6 16.0 %all-gather.1 = bf16[1024,256]{1,0:T(8,128)(2,1)S(1)} all-gather(bf16[256,256]{1,0:T(8,128)(2,1)S(1)} %add_convert_fusion.1), channel_id=3, replica_groups=mesh['ctx'=4,'fsdp'=8] {'ctx'}, dimensions={0}, use_global_device_ids=true | all-gather | bytes 655360 | tf_op jit(solution)/shard_map/all_gather | solution.py:1329
  103.6 0.8 copy.59
  104.4 16.5 %all-gather.2 = bf16[1024,256]{1,0:T(8,128)(2,1)S(1)} all-gather(bf16[256,256]{1,0:T(8,128)(2,1)S(1)} %slice.126), channel_id=4, replica_groups=mesh['ctx'=4,'fsdp'=8] {'ctx'}, dimensions={0}, use_global_device_ids=true | all-gather | bytes 655360 | tf_op jit(solution)/shard_map/all_gather | solution.py:1329
  120.9 0.8 copy.60
  121.7 2.9 copy.51
  124.6 1.8 slice_negate_fusion
  126.4 1.6 maximum_multiply_fusion
  127.9 2.9 copy.53
  130.8 4.4 add_convert_fusion.q_ref.q_in
  135.2 15.3 %attend.1 = (bf16[256,2048]{1,0:T(8,128)(2,1)}, f32[2,512,128]{2,1,0:T(8,128)}) custom-call(bf16[256,2048]{1,0:T(8,128)(2,1)} %add_convert_fusion.q_ref.q_in, bf16[1024,256]{1,0:T(8,128)(2,1)} %bitcast.81, bf16[1024,256]{1,0:T(8,128)(2,1)} %bitcast.83, f32[2,128,512]{2,1,0:T(8,128)} %compare_select_fusion.mask_ref.mask_in), custom_call_target="tpu_custom_call" | custom-call | flops 2147483648 | bytes 4194304 | tf_op jit(solution)/shard_map/attend/pallas_call | solution.py:138
  150.5 8.5 %multiply_reduce_fusion = (f32[256]{0:T(256)S(1)}, f32[256,8,256]{0,2,1:T(8,128)}) fusion(bf16[256,8,256]{0,2,1:T(8,128)(2,1)S(1)} %bitcast.86, bf16[128,8,256]{0,2,1:T(8,128)(2,1)S(1)} %bitcast.89, bf16[128,8,256]{0,2,1:T(8,128)(2,1)S(1)} %bitcast.90, pred[]{:T(512)} %bitcast, bf16[8,2048,256]{2,1,0:T(8,128)(2,1)} %bitcast.74, ...), kind=kOutput, calls=%fused_computation.11 | convolution fusion | flops 2152201984 | bytes 13632513 | tf_op jit(solution)/shard_map/dot_general | solution.py:1334
  158.9 2.9 copy.68
  161.9 4.3 multiply_convert_fusion
  166.2 23.5 %all-gather.8.cloned.1.call-done.cot_ref = bf16[8,256,2048]{2,1,0:T(8,128)(2,1)} async-done(((bf16[1,256,2048]{2,1,0:T(8,128)(2,1)}), bf16[8,256,2048]{2,1,0:T(8,128)(2,1)}) %all-gather.8.cloned.1.call-update) | async-done | bytes 8388624 | tf_op jit(solution)/shard_map/all_gather | solution.py:1339
  189.7 386.7 %back.1 = (bf16[256,2048]{1,0:T(8,128)(2,1)}, bf16[256,2048]{1,0:T(8,128)(2,1)}, f32[2,2048]{1,0:T(2,128)}, bf16[704,2048]{1,0:T(8,128)(2,1)}, bf16[704,2048]{1,...) custom-call(bf16[256,2048]{1,0:T(8,128)(2,1)} %get-tuple-element.66., ...), custom_call_target="tpu_custom_call" | custom-call | tf_op jit(solution)/shard_map/back/pallas_call | solution.py:1242
  576.4 1.8 fusion.20
  578.2 2.9 slice.116
  581.1 0.6 fusion.24
  581.7 0.2 convert_bitcast_fusion.2
  582.0 1.8 copy.66
  583.9 1.1 copy-done.4
  585.1 0.8 copy-done.6
  585.9 3.7 convert_element_type.64
  589.6 1.1 copy-done.8
  590.7 5.9 convert_bitcast_fusion
  596.6 2.1 fusion.8
  (67 shorter events, 1.5 us)
Async XLA Ops:
  7.2 3.5 copy-start.19
  7.2 5.5 copy-start.5
  7.2 69.3 %all-gather.10.cloned.1.call-start = ((), (), s32[]{:S(2)}) async-start(), calls=%async_computation.1 | async-start | bytes 11796480 | tf_op jit(solution)/shard_map/all_gather | solution.py:1310
  9.9 140.6 %all-gather.12.cloned.1.call-start = ((), (), s32[]{:S(2)}) async-start(), calls=%async_computation.2 | async-start | bytes 9437184 | tf_op jit(solution)/shard_map/all_gather | solution.py:1311
  10.6 179.1 %all-gather.8.cloned.1.call-start = ((), (), s32[]{:S(2)}) async-start(), calls=%async_computation | async-start | bytes 9437184 | tf_op jit(solution)/shard_map/all_gather | solution.py:1339
  14.1 2.1 copy-start
  19.9 2.9 copy-start.9
  19.9 2.9 copy-start.10
  22.0 54.5 %copy-start.17 = (f32[2048]{0:T(1024)S(1)}, f32[2048]{0:T(1024)}, u32[]{:S(2)}) copy-start(f32[2048]{0:T(1024)} %param.15) | copy-start | bytes 24580
  23.2 138.6 %copy-start.1 = (bf16[256,2048]{1,0:T(8,128)(2,1)}, bf16[256,2048]{1,0:T(8,128)(2,1)S(1)}, u32[]{:S(2)}) copy-start(bf16[256,2048]{1,0:T(8,128)(2,1)S(1)} %get-tuple-element.69.x_in) | copy-start | bytes 3145732
  82.6 1.5 copy-start.2
  85.6 1.0 copy-start.12
  135.2 15.3 %copy-start.13 = (bf16[1,256,2048]{1,2,0:T(8,128)(2,1)S(1)}, bf16[1,256,2048]{1,2,0:T(8,128)(2,1)}, u32[]{:S(2)}) copy-start(bf16[1,256,2048]{1,2,0:T(8,128)(2,1)} %copy.65) | copy-start | bytes 3145732
  135.2 15.3 %copy-start.14 = (bf16[1,128,2048]{1,2,0:T(8,128)(2,1)S(1)}, bf16[1,128,2048]{1,2,0:T(8,128)(2,1)}, u32[]{:S(2)}) copy-start(bf16[1,128,2048]{1,2,0:T(8,128)(2,1)} %copy.70) | copy-start | bytes 1572868
  135.2 15.3 %copy-start.15 = (bf16[1,128,2048]{1,2,0:T(8,128)(2,1)S(1)}, bf16[1,128,2048]{1,2,0:T(8,128)(2,1)}, u32[]{:S(2)}) copy-start(bf16[1,128,2048]{1,2,0:T(8,128)(2,1)} %copy.69) | copy-start | bytes 1572868
  158.9 2.9 copy-start.16
  578.2 2.9 copy-start.18
  578.2 3.5 copy-start.11
  581.9 1.8 copy-start.3
  583.8 1.2 copy-start.4
  583.8 2.1 copy-start.6
  585.9 3.7 copy-start.7
  585.9 4.8 copy-start.8
Sparse Core Ops, SparseCore 0:
  10.5 65.9 all-gather.9
  78.4 54.3 all-gather.11
  135.3 54.4 all-gather.7
